TPU v7x, 32 devices: a whole 2x2x4 slice. The times are simulated.
32 devices in a mesh: ca: 16 (over z, y, x), tp: 2 (over core).
Axes of the slice: x: 2, y: 2, z: 4, core: 2. Of those that a mesh axis runs over, the one named last changes fastest.
Arguments:
- tokens: bfloat16 [8192, 4096], P('ca'), may hold values from -7 to 7
- lengths: int32 [8], replicated, may hold values from 1 to 1536, 8192 in all
- w_query: bfloat16 [4096, 4096], P('ca', 'tp'), may hold values from -0.09375 to 0.09375
- w_key: bfloat16 [4096, 1024], P('ca', 'tp'), may hold values from -0.09375 to 0.09375
- w_value: bfloat16 [4096, 1024], P('ca', 'tp'), may hold values from -0.09375 to 0.09375
Outputs:
- attended: bfloat16 [8192, 4096], P('ca', 'tp')
Inputs may be any that keep to these rules, and one draw needn't show every extreme that they name: `lengths`: the 8 documents lie end to end in this order and fill all 8192 tokens; the longest has exactly 1536 tokens.
All inputs are finite; a program needn't handle non-finite values.
Results may differ from a plain program's by a relative error of at most 0.007.
Values may be sent and summed in bfloat16 or wider, within the bound.
No kernel may reach another device: no remote copies, remote signals or barrier semaphores. Data moves between devices by JAX's collectives and lax.ppermute only.
A program may use at most 64 MiB of HBM per device.

v0:
```python
import functools
import math

import jax
import jax.numpy as jnp
from jax import lax
from jax.experimental import pallas as pl
from jax.experimental.pallas import tpu as pltpu
from jax.sharding import PartitionSpec as P

HEADS = 32
KV_HEADS = 8
HEAD_DIM = 128
REACH = 3
ROPE_THETA = 500000.0
LOGIT_CAP = 5.0
TILE = 256
VMEM_BYTES = 48 * 1024 * 1024


def doc_starts(lengths, positions):
    doc_ends = jnp.cumsum(lengths).astype(jnp.int32)
    before = doc_ends[None, :] <= positions[:, None]
    return jnp.max(jnp.where(before, doc_ends[None, :], 0), axis=1).astype(jnp.int32)


def rope_tables(offsets):
    half_dim = HEAD_DIM // 2
    frequency = ROPE_THETA ** (-(jnp.arange(half_dim, dtype=jnp.float32) * 2.0) / HEAD_DIM)
    angles = offsets.astype(jnp.float32)[:, None] * frequency[None, :]
    cosine, sine = jnp.cos(angles), jnp.sin(angles)
    return jnp.concatenate([cosine, cosine], axis=1), jnp.concatenate([-sine, sine], axis=1)


def rotated(values, cosine, sine):
    return values * cosine + pltpu.roll(values, HEAD_DIM // 2, 1) * sine


def project_kernel(rope_heads, group, slice_rows, place, x_ref, own_ref, rest_ref, cos_ref, sin_ref, out_ref, w_ref):
    @pl.when(pl.program_id(0) == 0)
    def _():
        lines = own_ref.shape[0] // slice_rows
        mine = place[0]
        for line in range(lines):
            at = pl.multiple_of((line * group + mine) * slice_rows, slice_rows)
            w_ref[pl.ds(at, slice_rows), :] = own_ref[line * slice_rows : (line + 1) * slice_rows, :]
            for step in range(1, group):
                at = pl.multiple_of((line * group + (mine ^ step)) * slice_rows, slice_rows)
                first = (line * (group - 1) + step - 1) * slice_rows
                w_ref[pl.ds(at, slice_rows), :] = rest_ref[first : first + slice_rows, :]

    total = jnp.dot(x_ref[...], w_ref[...], preferred_element_type=jnp.float32)
    cosine, sine = cos_ref[...], sin_ref[...]
    for head in range(out_ref.shape[1] // HEAD_DIM):
        columns = slice(head * HEAD_DIM, (head + 1) * HEAD_DIM)
        part = total[:, columns]
        if head < rope_heads:
            part = rotated(part, cosine, sine)
        out_ref[:, columns] = part.astype(out_ref.dtype)


def project(place, tokens, own, rest, column_block, width, cosine, sine, rope_heads, group, slice_rows):
    rows, depth = tokens.shape
    tile = min(512, rows)
    if rest is None:
        rest = jnp.zeros((16, width), own.dtype)
    kernel = functools.partial(project_kernel, rope_heads, group, slice_rows)
    return pl.pallas_call(
        kernel,
        out_shape=jax.ShapeDtypeStruct((rows, width), jnp.bfloat16),
        grid_spec=pltpu.PrefetchScalarGridSpec(
            num_scalar_prefetch=1,
            grid=(rows // tile,),
            in_specs=[
                pl.BlockSpec((tile, depth), lambda i, s: (i, 0)),
                pl.BlockSpec((own.shape[0], width), lambda i, s: (0, column_block)),
                pl.BlockSpec(rest.shape, lambda i, s: (0, 0)),
                pl.BlockSpec((tile, HEAD_DIM), lambda i, s: (i, 0)),
                pl.BlockSpec((tile, HEAD_DIM), lambda i, s: (i, 0)),
            ],
            out_specs=pl.BlockSpec((tile, width), lambda i, s: (i, 0)),
            scratch_shapes=[pltpu.VMEM((depth, width), own.dtype)],
        ),
        compiler_params=pltpu.CompilerParams(vmem_limit_bytes=VMEM_BYTES),
        cost_estimate=pl.CostEstimate(
            flops=2 * rows * depth * width, bytes_accessed=2 * depth * (rows + width), transcendentals=0
        ),
    )(place, tokens, own, rest, cosine, sine)


def attend_kernel(kv_heads, share, halo_rows, bounds, q_ref, start_ref, halo_ref, kv_ref, out_ref, kv_all, sums, totals):
    tile_index = pl.program_id(0)

    @pl.when(tile_index == 0)
    def _():
        kv_all[:halo_rows, :] = halo_ref[...]
        kv_all[halo_rows:, :] = kv_ref[...]

    tile = q_ref.shape[0]
    place = bounds[0, tile_index]
    first_start = bounds[1, tile_index]
    last_start = bounds[2, tile_index]
    q_first = halo_rows + place
    first_block = first_start // TILE
    last_block = (q_first + tile - 1) // TILE
    sums[...] = jnp.zeros_like(sums)
    totals[...] = jnp.zeros_like(totals)
    inner = 1.0 / (math.sqrt(HEAD_DIM) * LOGIT_CAP)
    outer = LOGIT_CAP * math.log2(math.e)

    def block_step(block, masked):
        rows = pl.ds(pl.multiple_of(block * TILE, TILE), TILE)
        if masked:
            k_ids = block * TILE + lax.broadcasted_iota(jnp.int32, (tile, TILE), 1)
            q_ids = q_first + lax.broadcasted_iota(jnp.int32, (tile, TILE), 0)
            allowed = (k_ids <= q_ids) & (k_ids >= start_ref[...])
        for kv_head in range(kv_heads):
            keys = kv_all[rows, kv_head * HEAD_DIM : (kv_head + 1) * HEAD_DIM]
            at = (kv_heads + kv_head) * HEAD_DIM
            values = kv_all[rows, at : at + HEAD_DIM]
            for member in range(share):
                head = kv_head * share + member
                query = q_ref[:, head * HEAD_DIM : (head + 1) * HEAD_DIM]
                raw = lax.dot_general(query, keys, (((1,), (1,)), ((), ())), preferred_element_type=jnp.float32)
                weights = jnp.exp2(outer * jnp.tanh(raw * inner))
                if masked:
                    weights = jnp.where(allowed, weights, 0.0)
                partial = weights[:, :HEAD_DIM]
                for part in range(1, TILE // HEAD_DIM):
                    partial = partial + weights[:, part * HEAD_DIM : (part + 1) * HEAD_DIM]
                totals[head] += partial
                sums[head] += jnp.dot(weights.astype(jnp.bfloat16), values, preferred_element_type=jnp.float32)

    def either(block, carry):
        begin = block * TILE
        whole = (begin >= last_start) & (begin + TILE - 1 <= q_first)

        @pl.when(whole)
        def _():
            block_step(block, False)

        @pl.when(jnp.logical_not(whole))
        def _():
            block_step(block, True)

        return carry

    lax.fori_loop(first_block, last_block + 1, either, 0)
    for head in range(kv_heads * share):
        denominator = jnp.sum(totals[head], axis=1, keepdims=True)
        out_ref[:, head * HEAD_DIM : (head + 1) * HEAD_DIM] = (sums[head] / denominator).astype(out_ref.dtype)


def attend(chunk, chunk_rows, query, starts, halo, kv, kv_heads):
    width = query.shape[1]
    heads = width // HEAD_DIM
    halo_rows = halo.shape[0]
    tiles = chunk_rows // TILE
    places = chunk * chunk_rows + jnp.arange(tiles, dtype=jnp.int32) * TILE
    bounds = jnp.stack([places, starts[places], starts[places + TILE - 1]])
    kernel = functools.partial(attend_kernel, kv_heads, heads // kv_heads, halo_rows)
    return pl.pallas_call(
        kernel,
        out_shape=jax.ShapeDtypeStruct((chunk_rows, width), jnp.bfloat16),
        grid_spec=pltpu.PrefetchScalarGridSpec(
            num_scalar_prefetch=1,
            grid=(tiles,),
            in_specs=[
                pl.BlockSpec((TILE, width), lambda i, s: (s[0, i] // TILE, 0)),
                pl.BlockSpec((TILE, 1), lambda i, s: (s[0, i] // TILE, 0)),
                pl.BlockSpec(halo.shape, lambda i, s: (0, 0)),
                pl.BlockSpec(kv.shape, lambda i, s: (0, 0)),
            ],
            out_specs=pl.BlockSpec((TILE, width), lambda i, s: (i, 0)),
            scratch_shapes=[
                pltpu.VMEM((halo_rows + kv.shape[0], kv.shape[1]), jnp.bfloat16),
                pltpu.VMEM((heads, TILE, HEAD_DIM), jnp.float32),
                pltpu.VMEM((heads, TILE, HEAD_DIM), jnp.float32),
            ],
        ),
        compiler_params=pltpu.CompilerParams(vmem_limit_bytes=VMEM_BYTES),
        cost_estimate=pl.CostEstimate(
            flops=4 * chunk_rows * width * (halo_rows + chunk_rows) // 2,
            bytes_accessed=4 * chunk_rows * width,
            transcendentals=chunk_rows * heads * (halo_rows + chunk_rows),
        ),
    )(bounds, query, starts[:, None], halo, kv)


def per_device(group, lines, cores, tokens, lengths, w_query, w_key, w_value):
    row_count, depth = tokens.shape
    slice_rows = w_query.shape[0]
    index = lax.axis_index("ca")
    mine, line = index % group, index // group
    core = lax.axis_index("tp")
    q_width = w_query.shape[1] // group
    one_width = w_key.shape[1] // group
    kv_width = 2 * one_width
    kv_heads = one_width // HEAD_DIM
    group_rows = group * row_count
    devices = range(group * lines)

    def slice_for(target):
        return jnp.concatenate(
            [
                lax.dynamic_slice_in_dim(w_query, target * q_width, q_width, 1),
                lax.dynamic_slice_in_dim(w_key, target * one_width, one_width, 1),
                lax.dynamic_slice_in_dim(w_value, target * one_width, one_width, 1),
            ],
            axis=1,
        )

    def to_partner(block, step):
        return lax.ppermute(block, "ca", [(i, i ^ step) for i in devices])

    def along_lines(block):
        lanes = [[place + group * i for i in range(lines)] for place in range(group)]
        return lax.all_gather(block, "ca", axis=0, tiled=True, axis_index_groups=lanes)

    own_slices = along_lines(slice_for(mine))
    rest_kv = rest_q = None
    all_tokens = tokens
    if group > 1:
        arrived = [to_partner(slice_for(mine ^ step), step) for step in range(1, group)]
        rest_kv = along_lines(jnp.concatenate([a[:, q_width:] for a in arrived]))
        rest_q = along_lines(jnp.concatenate([a[:, :q_width] for a in arrived]))

        half = row_count // cores
        both = ("ca", "tp")

        def cross(block, steps):
            pairs = [(i * 2 + c, (i ^ steps[c]) * 2 + c) for i in devices for c in range(2)]
            return lax.ppermute(block, both, pairs)

        def swap(block):
            return lax.ppermute(block, both, [(i * 2 + c, i * 2 + 1 - c) for i in devices for c in range(2)])

        own_half = lax.dynamic_slice_in_dim(tokens, core * half, half, 0)
        near = cross(own_half, (1, 2))
        other = cross(own_half, (2, 1))
        far = cross(near, (2, 1))
        all_tokens = jnp.zeros((group_rows, depth), tokens.dtype)
        all_tokens = lax.dynamic_update_slice_in_dim(all_tokens, tokens, mine * row_count, 0)
        for block, steps in ((near, (1, 2)), (other, (2, 1)), (far, (3, 3))):
            mate = swap(block)
            step_here = jnp.where(core == 0, steps[0], steps[1])
            step_mate = jnp.where(core == 0, steps[1], steps[0])
            all_tokens = lax.dynamic_update_slice_in_dim(
                all_tokens, block, (mine ^ step_here) * row_count + core * half, 0
            )
            all_tokens = lax.dynamic_update_slice_in_dim(
                all_tokens, mate, (mine ^ step_mate) * row_count + (1 - core) * half, 0
            )

    row_ids = line * group_rows + jnp.arange(group_rows, dtype=jnp.int32)
    starts = doc_starts(lengths, row_ids)
    cosine, sine = rope_tables(row_ids - starts)
    place = mine.reshape(1).astype(jnp.int32)
    kv = project(
        place, all_tokens, own_slices, rest_kv, q_width // kv_width, kv_width, cosine, sine, kv_heads, group, slice_rows
    )
    query = project(
        place, all_tokens, own_slices, rest_q, 0, q_width, cosine, sine, q_width // HEAD_DIM, group, slice_rows
    )

    halo_rows = REACH * row_count
    hops = -(-halo_rows // group_rows)
    pieces, moving = [], kv
    for hop in range(hops):
        keep = min(halo_rows - hop * group_rows, group_rows)
        moving = moving[moving.shape[0] - keep :]
        moving = lax.ppermute(moving, "ca", [(i, i + group) for i in devices if i + group in devices])
        pieces.insert(0, moving)
    halo = pieces[0] if len(pieces) == 1 else jnp.concatenate(pieces)

    window_starts = starts - (line * group_rows - halo_rows)
    result = jnp.zeros((row_count, w_query.shape[1]), jnp.bfloat16)
    for step in reversed(range(group)):
        part = attend(mine ^ step, row_count, query, window_starts, halo, kv, kv_heads)
        if step > 0:
            part = to_partner(part, step)
        elif group == 1:
            return part
        result = lax.dynamic_update_slice_in_dim(result, part, (mine ^ step) * q_width, 1)
    return result


def solution(mesh):
    size, cores = mesh.shape["ca"], mesh.shape["tp"]
    local_kv = KV_HEADS // cores
    group = 4 if cores == 2 and local_kv % 4 == 0 and size % 4 == 0 else 1
    placed = (P("ca", None), P(), P("ca", "tp"), P("ca", "tp"), P("ca", "tp"))
    body = functools.partial(per_device, group, size // group, cores)
    return jax.shard_map(body, mesh=mesh, in_specs=placed, out_specs=P("ca", "tp"), check_vma=False)
```

profile of v0, /device:TPU:10, one launch (start us, length us, event | category | flops | bytes accessed | tf_op | source)
XLA Modules:
  0.0 225.5 jit_solution(15428223663540050848)
XLA Ops:
  6.5 1.3 constant_dynamic-slice_fusion.8
  9.6 1.6 collective-permute-start.7
  11.2 1.5 collective-permute-start.8
  12.7 3.1 %constant_dynamic-slice_fusion.12 = bf16[256,4096]{1,0:T(8,128)(2,1)} fusion(bf16[512,4096]{1,0:T(8,128)(2,1)} %param.5, s32[]{:T(128)S(6)} %select_n.166), kind=kLoop, calls=%fused_computation.44 | loop fusion | bytes 4194308 | tf_op jit(solution)/shard_map/dynamic_slice | solution.py:238
  16.4 1.5 collective-permute-start.2
  17.9 3.1 %collective-permute-done.6 = bf16[256,768]{1,0:T(8,128)(2,1)S(1)} collective-permute-done((bf16[256,768]{1,0:T(8,128)(2,1)S(1)}, bf16[256,768]{1,0:T(8,128)(2,1)S(1)}, u32[]{:S(2)}, u32[]{:S(2)}) %collective-permute-start.6) | collective-permute-done | bytes 393248 | tf_op jit(solution)/shard_map/ppermute | solution.py:214
  21.0 8.8 %collective-permute-done.7 = bf16[256,768]{1,0:T(8,128)(2,1)S(1)} collective-permute-done((bf16[256,768]{1,0:T(8,128)(2,1)S(1)}, bf16[256,768]{1,0:T(8,128)(2,1)S(1)}, u32[]{:S(2)}, u32[]{:S(2)}) %collective-permute-start.7) | collective-permute-done | bytes 393248 | tf_op jit(solution)/shard_map/ppermute | solution.py:214
  31.8 41.6 %collective-permute-done = bf16[256,4096]{1,0:T(8,128)(2,1)} collective-permute-done((bf16[256,4096]{1,0:T(8,128)(2,1)}, bf16[256,4096]{1,0:T(8,128)(2,1)}, u32[]{:S(2)}, u32[]{:S(2)}) %collective-permute-start) | collective-permute-done | bytes 2097184 | tf_op jit(solution)/shard_map/ppermute | solution.py:233
  73.4 1.5 collective-permute-start.4
  79.9 3.7 %fusion = (f32[2048,64]{1,0:T(8,128)S(1)}, f32[2048,64]{1,0:T(8,128)S(1)}, f32[2048,64]{1,0:T(8,128)S(1)}) fusion(f32[64]{0:T(128)S(1)} %multiply_power_fusion, f32[2048]{0:T(1024)S(1)} %get-tuple-element.20), kind=kLoop, calls=%fused_computation.18 | loop fusion | flops 262144 | bytes 1581312 | tf_op jit(solution)/shard_map/neg | solution.py:32
  84.9 1.3 copy.10.start_ref
  87.5 7.4 %broadcast_in_dim.16 = bf16[2048,4096]{1,0:T(8,128)(2,1)} broadcast(bf16[]{:T(256)} %constant.62.clone.1), dimensions={} | broadcast | bytes 16777218 | tf_op jit(solution)/shard_map/broadcast_in_dim | solution.py:242
  94.9 2.3 %constant_dynamic-update-slice_fusion.10 = bf16[2048,4096]{1,0:T(8,128)(2,1)} fusion(bf16[2048,4096]{1,0:T(8,128)(2,1)} %broadcast_in_dim.16, bf16[512,4096]{1,0:T(8,128)(2,1)S(1)} %copy-done.3, s32[]{:T(128)S(6)} %select_n.165), kind=kLoop, calls=%fused_computation.45 | loop fusion | bytes 8388612 | tf_op jit(solution)/shard_map/dynamic_update_slice | solution.py:243
  97.1 2.6 %collective-permute-done.4 = bf16[256,4096]{1,0:T(8,128)(2,1)} collective-permute-done((bf16[256,4096]{1,0:T(8,128)(2,1)}, bf16[256,4096]{1,0:T(8,128)(2,1)}, u32[]{:S(2)}, u32[]{:S(2)}) %collective-permute-start.4) | collective-permute-done | bytes 2097184 | tf_op jit(solution)/shard_map/ppermute | solution.py:233
  99.7 3.2 %constant_dynamic-update-slice_fusion.9 = bf16[2048,4096]{1,0:T(8,128)(2,1)} fusion(bf16[2048,4096]{1,0:T(8,128)(2,1)} %constant_dynamic-update-slice_fusion.10, bf16[256,4096]{1,0:T(8,128)(2,1)} %collective-permute-done, s32[]{:T(128)S(6)} %select_n.168), kind=kLoop, calls=%fused_computation.43 | loop fusion | bytes 4194308 | tf_op jit(solution)/shard_map/dynamic_update_slice | solution.py:248
  103.0 3.1 %constant_dynamic-update-slice_fusion.8 = bf16[2048,4096]{1,0:T(8,128)(2,1)} fusion(bf16[2048,4096]{1,0:T(8,128)(2,1)} %constant_dynamic-update-slice_fusion.9, bf16[256,4096]{1,0:T(8,128)(2,1)} %collective-permute-done.1, s32[]{:T(128)S(6)} %select_n.170), kind=kLoop, calls=%fused_computation.42 | loop fusion | bytes 4194308 | tf_op jit(solution)/shard_map/dynamic_update_slice | solution.py:251
  106.1 3.1 %constant_dynamic-update-slice_fusion.7 = bf16[2048,4096]{1,0:T(8,128)(2,1)} fusion(bf16[2048,4096]{1,0:T(8,128)(2,1)} %constant_dynamic-update-slice_fusion.8, bf16[256,4096]{1,0:T(8,128)(2,1)} %collective-permute-done.2, s32[]{:T(128)S(6)} %select_n.171), kind=kLoop, calls=%fused_computation.41 | loop fusion | bytes 4194308 | tf_op jit(solution)/shard_map/dynamic_update_slice | solution.py:248
  109.2 3.1 %constant_dynamic-update-slice_fusion.6 = bf16[2048,4096]{1,0:T(8,128)(2,1)} fusion(bf16[2048,4096]{1,0:T(8,128)(2,1)} %constant_dynamic-update-slice_fusion.7, bf16[256,4096]{1,0:T(8,128)(2,1)} %collective-permute-done.3, s32[]{:T(128)S(6)} %select_n.172), kind=kLoop, calls=%fused_computation.40 | loop fusion | bytes 4194308 | tf_op jit(solution)/shard_map/dynamic_update_slice | solution.py:251
  112.3 3.2 %constant_dynamic-update-slice_fusion.5 = bf16[2048,4096]{1,0:T(8,128)(2,1)} fusion(bf16[2048,4096]{1,0:T(8,128)(2,1)} %constant_dynamic-update-slice_fusion.6, bf16[256,4096]{1,0:T(8,128)(2,1)} %collective-permute-done.4, s32[]{:T(128)S(6)} %select_n.173), kind=kLoop, calls=%fused_computation.39 | loop fusion | bytes 4194308 | tf_op jit(solution)/shard_map/dynamic_update_slice | solution.py:248
  115.6 1.5 constant_dynamic-update-slice_fusion.4.x_ref
  117.1 1.4 copy-done
  118.5 9.2 %shard_map.56.kv_ref = bf16[2048,256]{1,0:T(8,128)(2,1)S(1)} custom-call(s32[1]{0:T(128)} %bitcast.6.place, bf16[2048,4096]{1,0:T(8,128)(2,1)} %constant_dynamic-update-slice_fusion.4.x_ref, bf16[1024,768]{1,0:T(8,128)(2,1)S(1)} %copy-done, bf16[3072,256]{1,0:T(8,128)(2,1)} %all-gather.8.cloned.1.call-done.rest_ref, ...), custom_call_target="tpu_custom_call" | custom-call | flops 4294967296 | bytes 18874368 | tf_op jit(solution)/shard_map/pallas_call | solution.py:68
  128.7 3.6 %collective-permute-start.9 = (bf16[1536,256]{1,0:T(8,128)(2,1)}, bf16[1536,256]{1,0:T(8,128)(2,1)}, u32[]{:S(2)}, u32[]{:S(2)}) collective-permute-start(bf16[1536,256]{1,0:T(8,128)(2,1)} %slice.50), channel_id=1, source_target_pairs={{0,8},{2,10},{4,12},{6,14},{8,16},{10,18},{12,20},{14,22},{16,24},... | collective-permute-start | bytes 2359304 | tf_op jit(solution)/shard_map/ppermute | solution.py:272
  132.4 26.1 %all-gather.6.cloned.1.call-done.rest_ref = bf16[3072,512]{1,0:T(8,128)(2,1)} async-done(((bf16[768,512]{1,0:T(8,128)(2,1)}), bf16[3072,512]{1,0:T(8,128)(2,1)}) %all-gather.6.cloned.1.call-update) | async-done | bytes 3145744 | tf_op jit(solution)/shard_map/all_gather | solution.py:218
  158.5 1.4 copy-done.1
  159.9 13.8 %shard_map.55.q_ref = bf16[2048,512]{1,0:T(8,128)(2,1)S(1)} custom-call(s32[1]{0:T(128)} %bitcast.6.place, bf16[2048,4096]{1,0:T(8,128)(2,1)} %constant_dynamic-update-slice_fusion.4.x_ref, bf16[1024,768]{1,0:T(8,128)(2,1)S(1)} %copy-done.1, bf16[3072,512]{1,0:T(8,128)(2,1)} %all-gather.6.cloned.1.call-done.rest_ref, ...), custom_call_target="tpu_custom_call" | custom-call | flops 8589934592 | bytes 20971520 | tf_op jit(solution)/shard_map/pallas_call | solution.py:68
  173.7 8.8 %shard_map.57 = bf16[512,512]{1,0:T(8,128)(2,1)S(1)} custom-call(s32[3,2]{1,0:T(4,128)S(1)} %get-tuple-element.22.bounds, bf16[2048,512]{1,0:T(8,128)(2,1)S(1)} %shard_map.55.q_ref, s32[2048,1]{1,0:T(8,128)S(1)} %copy-done.2, bf16[1536,256]{1,0:T(8,128)(2,1)} %collective-permute-done.9.halo_ref, bf16[2048,256]{1,0:T(8,128)(2,1)S(1)} %shard_map.56.kv_ref), custom_call_target="tpu_custom_call" | custom-call | flops 1073741824 | bytes 1048576 | tf_op jit(solution)/shard_map/pallas_call | solution.py:162
  182.7 11.8 %shard_map.58 = bf16[512,512]{1,0:T(8,128)(2,1)S(1)} custom-call(s32[3,2]{1,0:T(4,128)S(1)} %get-tuple-element.23.bounds, bf16[2048,512]{1,0:T(8,128)(2,1)S(1)} %shard_map.55.q_ref, s32[2048,1]{1,0:T(8,128)S(1)} %copy-done.2, bf16[1536,256]{1,0:T(8,128)(2,1)} %collective-permute-done.9.halo_ref, bf16[2048,256]{1,0:T(8,128)(2,1)S(1)} %shard_map.56.kv_ref), custom_call_target="tpu_custom_call" | custom-call | flops 1073741824 | bytes 1048576 | tf_op jit(solution)/shard_map/pallas_call | solution.py:162
  194.5 8.9 %shard_map.59 = bf16[512,512]{1,0:T(8,128)(2,1)S(1)} custom-call(s32[3,2]{1,0:T(4,128)S(1)} %pad_add_fusion.2.bounds, bf16[2048,512]{1,0:T(8,128)(2,1)S(1)} %shard_map.55.q_ref, s32[2048,1]{1,0:T(8,128)S(1)} %copy-done.2, bf16[1536,256]{1,0:T(8,128)(2,1)} %collective-permute-done.9.halo_ref, bf16[2048,256]{1,0:T(8,128)(2,1)S(1)} %shard_map.56.kv_ref), custom_call_target="tpu_custom_call" | custom-call | flops 1073741824 | bytes 1048576 | tf_op jit(solution)/shard_map/pallas_call | solution.py:162
  203.6 6.1 %shard_map.60 = bf16[512,512]{1,0:T(8,128)(2,1)S(1)} custom-call(s32[3,2]{1,0:T(4,128)S(1)} %pad_add_fusion.3.bounds, bf16[2048,512]{1,0:T(8,128)(2,1)S(1)} %shard_map.55.q_ref, s32[2048,1]{1,0:T(8,128)S(1)} %copy-done.2, bf16[1536,256]{1,0:T(8,128)(2,1)} %collective-permute-done.9.halo_ref, bf16[2048,256]{1,0:T(8,128)(2,1)S(1)} %shard_map.56.kv_ref), custom_call_target="tpu_custom_call" | custom-call | flops 1073741824 | bytes 1048576 | tf_op jit(solution)/shard_map/pallas_call | solution.py:162
  210.1 6.7 %collective-permute-done.12 = bf16[512,512]{1,0:T(8,128)(2,1)S(1)} collective-permute-done((bf16[512,512]{1,0:T(8,128)(2,1)S(1)}, bf16[512,512]{1,0:T(8,128)(2,1)S(1)}, u32[]{:S(2)}, u32[]{:S(2)}) %collective-permute-start.12) | collective-permute-done | bytes 524320 | tf_op jit(solution)/shard_map/ppermute | solution.py:214
  216.8 1.3 copy-done.4
  (91 shorter events, 14.0 us)
Async XLA Ops:
  6.5 1.4 copy-start.6
  6.5 1.4 copy-start.5
  6.5 110.5 %all-gather.4.cloned.1.call-start = ((), (), s32[]{:S(2)}) async-start(), calls=%async_computation | async-start | bytes 1966080 | tf_op jit(solution)/shard_map/all_gather | solution.py:218
  8.9 108.2 %all-gather.8.cloned.1.call-start = ((), (), s32[]{:S(2)}) async-start(), calls=%async_computation.2 | async-start | bytes 1966080 | tf_op jit(solution)/shard_map/all_gather | solution.py:218
  9.0 12.1 %collective-permute-start.6 = (bf16[256,768]{1,0:T(8,128)(2,1)S(1)}, bf16[256,768]{1,0:T(8,128)(2,1)S(1)}, u32[]{:S(2)}, u32[]{:S(2)}) collective-permute-start(bf16[256,768]{1,0:T(8,128)(2,1)S(1)} %pad_maximum_fusion.4), channel_id=1, source_target_pairs={{0,2},{2,0},{4,6},{6,4},{8,10},{10,8},{12,14},{14,12},{16,18},{18,... | collective-permute-start | bytes 1179656 | tf_op jit(solution)/shard_map/ppermute | solution.py:214
  9.6 20.2 %collective-permute-start.7 = (bf16[256,768]{1,0:T(8,128)(2,1)S(1)}, bf16[256,768]{1,0:T(8,128)(2,1)S(1)}, u32[]{:S(2)}, u32[]{:S(2)}) collective-permute-start(bf16[256,768]{1,0:T(8,128)(2,1)S(1)} %pad_maximum_fusion.5), channel_id=1, source_target_pairs={{0,4},{2,6},{4,0},{6,2},{8,12},{10,14},{12,8},{14,10},{16,20},{18,... | collective-permute-start | bytes 1179656 | tf_op jit(solution)/shard_map/ppermute | solution.py:214
  11.2 19.2 %collective-permute-start.8 = (bf16[256,768]{1,0:T(8,128)(2,1)S(1)}, bf16[256,768]{1,0:T(8,128)(2,1)S(1)}, u32[]{:S(2)}, u32[]{:S(2)}) collective-permute-start(bf16[256,768]{1,0:T(8,128)(2,1)S(1)} %pad_maximum_fusion.6), channel_id=1, source_target_pairs={{0,6},{2,4},{4,2},{6,0},{8,14},{10,12},{12,10},{14,8},{16,22},{18,... | collective-permute-start | bytes 1179656 | tf_op jit(solution)/shard_map/ppermute | solution.py:214
  12.7 18.7 %copy-start.7 = (s32[8]{0:T(128)S(1)}, s32[8]{0:T(128)}, u32[]{:S(2)}) copy-start(s32[8]{0:T(128)} %param.6) | copy-start | bytes 100
  15.9 57.5 %collective-permute-start = (bf16[256,4096]{1,0:T(8,128)(2,1)}, bf16[256,4096]{1,0:T(8,128)(2,1)}, u32[]{:S(2)}, u32[]{:S(2)}) collective-permute-start(bf16[256,4096]{1,0:T(8,128)(2,1)} %constant_dynamic-slice_fusion.12), channel_id=1, source_target_pairs={{0,2},{1,5},{2,0},{3,7},{4,6},{5,1},{6,4},{7,3},{8,10},{9,13},{10,... | collective-permute-start | bytes 6291464 | tf_op jit(solution)/shard_map/ppermute | solution.py:233
  16.4 67.8 %collective-permute-start.2 = (bf16[256,4096]{1,0:T(8,128)(2,1)}, bf16[256,4096]{1,0:T(8,128)(2,1)}, u32[]{:S(2)}, u32[]{:S(2)}) collective-permute-start(bf16[256,4096]{1,0:T(8,128)(2,1)} %constant_dynamic-slice_fusion.12), channel_id=1, source_target_pairs={{0,4},{1,3},{2,6},{3,1},{4,0},{5,7},{6,2},{7,5},{8,12},{9,11},{10,... | collective-permute-start | bytes 6291464 | tf_op jit(solution)/shard_map/ppermute | solution.py:233
  31.3 127.2 %all-gather.6.cloned.1.call-start = ((), (), s32[]{:S(2)}) async-start(), calls=%async_computation.1 | async-start | bytes 3932160 | tf_op jit(solution)/shard_map/all_gather | solution.py:218
  73.4 26.4 %collective-permute-start.4 = (bf16[256,4096]{1,0:T(8,128)(2,1)}, bf16[256,4096]{1,0:T(8,128)(2,1)}, u32[]{:S(2)}, u32[]{:S(2)}) collective-permute-start(bf16[256,4096]{1,0:T(8,128)(2,1)} %collective-permute-done), channel_id=1, source_target_pairs={{0,4},{1,3},{2,6},{3,1},{4,0},{5,7},{6,2},{7,5},{8,12},{9,11},{10,... | collective-permute-start | bytes 6291464 | tf_op jit(solution)/shard_map/ppermute | solution.py:233
  78.8 24.1 %collective-permute-start.1 = (bf16[256,4096]{1,0:T(8,128)(2,1)}, bf16[256,4096]{1,0:T(8,128)(2,1)}, u32[]{:S(2)}, u32[]{:S(2)}) collective-permute-start(bf16[256,4096]{1,0:T(8,128)(2,1)} %collective-permute-done), channel_id=1, source_target_pairs={{0,1},{1,0},{2,3},{3,2},{4,5},{5,4},{6,7},{7,6},{8,9},{9,8},{10,11... | collective-permute-start | bytes 6291464 | tf_op jit(solution)/shard_map/ppermute | solution.py:236
  84.2 25.0 %collective-permute-start.3 = (bf16[256,4096]{1,0:T(8,128)(2,1)}, bf16[256,4096]{1,0:T(8,128)(2,1)}, u32[]{:S(2)}, u32[]{:S(2)}) collective-permute-start(bf16[256,4096]{1,0:T(8,128)(2,1)} %collective-permute-done.2), channel_id=1, source_target_pairs={{0,1},{1,0},{2,3},{3,2},{4,5},{5,4},{6,7},{7,6},{8,9},{9,8},{10,11... | collective-permute-start | bytes 6291464 | tf_op jit(solution)/shard_map/ppermute | solution.py:236
  87.5 7.4 %copy-start.3 = (bf16[512,4096]{1,0:T(8,128)(2,1)S(1)}, bf16[512,4096]{1,0:T(8,128)(2,1)}, u32[]{:S(2)}) copy-start(bf16[512,4096]{1,0:T(8,128)(2,1)} %param.5) | copy-start | bytes 12582916
  99.7 15.8 %collective-permute-start.5 = (bf16[256,4096]{1,0:T(8,128)(2,1)}, bf16[256,4096]{1,0:T(8,128)(2,1)S(1)}, u32[]{:S(2)}, u32[]{:S(2)}) collective-permute-start(bf16[256,4096]{1,0:T(8,128)(2,1)} %collective-permute-done.4), channel_id=1, source_target_pairs={{0,1},{1,0},{2,3},{3,2},{4,5},{5,4},{6,7},{7,6},{8,9},{9,8},{10,11... | collective-permute-start | bytes 6291464 | tf_op jit(solution)/shard_map/ppermute | solution.py:236
  117.1 1.4 copy-start
  128.7 45.0 %collective-permute-start.9 = (bf16[1536,256]{1,0:T(8,128)(2,1)}, bf16[1536,256]{1,0:T(8,128)(2,1)}, u32[]{:S(2)}, u32[]{:S(2)}) collective-permute-start(bf16[1536,256]{1,0:T(8,128)(2,1)} %slice.50), channel_id=1, source_target_pairs={{0,8},{2,10},{4,12},{6,14},{8,16},{10,18},{12,20},{14,22},{16,24},... | collective-permute-start | bytes 2359304 | tf_op jit(solution)/shard_map/ppermute | solution.py:272
  158.5 1.4 copy-start.1
  159.9 13.8 %copy-start.2 = (s32[2048,1]{1,0:T(8,128)S(1)}, s32[2048,1]{1,0:T(8,128)}, u32[]{:S(2)}) copy-start(s32[2048,1]{1,0:T(8,128)} %copy.10.start_ref) | copy-start | bytes 24580
  182.6 27.1 %collective-permute-start.10 = (bf16[512,512]{1,0:T(8,128)(2,1)S(1)}, bf16[512,512]{1,0:T(8,128)(2,1)S(1)}, u32[]{:S(2)}, u32[]{:S(2)}) collective-permute-start(bf16[512,512]{1,0:T(8,128)(2,1)S(1)} %shard_map.57), channel_id=1, source_target_pairs={{0,6},{2,4},{4,2},{6,0},{8,14},{10,12},{12,10},{14,8},{16,22},{18,... | collective-permute-start | bytes 1572872 | tf_op jit(solution)/shard_map/ppermute | solution.py:214
  194.5 15.5 %collective-permute-start.11 = (bf16[512,512]{1,0:T(8,128)(2,1)S(1)}, bf16[512,512]{1,0:T(8,128)(2,1)S(1)}, u32[]{:S(2)}, u32[]{:S(2)}) collective-permute-start(bf16[512,512]{1,0:T(8,128)(2,1)S(1)} %shard_map.58), channel_id=1, source_target_pairs={{0,4},{2,6},{4,0},{6,2},{8,12},{10,14},{12,8},{14,10},{16,20},{18,... | collective-permute-start | bytes 1572872 | tf_op jit(solution)/shard_map/ppermute | solution.py:214
  203.5 13.2 %collective-permute-start.12 = (bf16[512,512]{1,0:T(8,128)(2,1)S(1)}, bf16[512,512]{1,0:T(8,128)(2,1)S(1)}, u32[]{:S(2)}, u32[]{:S(2)}) collective-permute-start(bf16[512,512]{1,0:T(8,128)(2,1)S(1)} %shard_map.59), channel_id=1, source_target_pairs={{0,2},{2,0},{4,6},{6,4},{8,10},{10,8},{12,14},{14,12},{16,18},{18,... | collective-permute-start | bytes 1572872 | tf_op jit(solution)/shard_map/ppermute | solution.py:214
  216.8 1.3 copy-start.4
Sparse Core Ops, SparseCore 0:
  9.0 37.2 all-gather.3
  47.8 35.9 all-gather.7
  85.4 73.0 all-gather.5
where the time goes:
time: 230 us; the launch traced here: 225 us
  waiting for transfers between devices  89.5 us (39%)
  Pallas kernels  58.7 us (26%)
  local copies, waits for them, and re-layouts  44.4 us (19%)
  between operations  13.6 us (6%)
  starting transfers between devices  11.8 us (5%)
  other arithmetic  7.42 us (3%)
    ppermute x3, waiting for transfers between devices, cross(): return lax.ppermute(block, both, pairs)  44.2 us
    pallas_call x4, Pallas kernels, attend(): pl.pallas_call(kernel, out_shape=jax.ShapeDtypeStruct((chunk_rows, width)...  35.6 us
    all_gather x3, waiting for transfers between devices, along_lines(): lax.all_gather(block, 'ca', axis=0, tiled=True, axis_index_groups=lanes)  26.1 us
    pallas_call x2, Pallas kernels, project(): pl.pallas_call(kernel, out_shape=jax.ShapeDtypeStruct((rows, width), jnp....  23 us
    ppermute x6, waiting for transfers between devices, to_partner(): return lax.ppermute(block, 'ca', [(i, i ^ step) for i in devices])  19.1 us
    dynamic_update_slice x3, local copies, waits for them, and re-layouts, per_device(): lax.dynamic_update_slice_in_dim(all_tokens, block, (mine ^ step_here) * r...  9.53 us
    dynamic_update_slice x3, local copies, waits for them, and re-layouts, per_device(): lax.dynamic_update_slice_in_dim(all_tokens, mate, (mine ^ step_mate) * ro...  7.77 us
    broadcast_in_dim x1, local copies, waits for them, and re-layouts, per_device(): all_tokens = jnp.zeros((group_rows, depth), tokens.dtype)  7.39 us
  transfers between devices with their start and end apart: 16, of which 7 were waited for; matrix products, arithmetic and copies ran while one was open for 20% of the time, Pallas kernels for 22%

commit v1 on v0

--- a/solution.py
+++ b/solution.py
@@ -36,56 +36,81 @@
     return values * cosine + pltpu.roll(values, HEAD_DIM // 2, 1) * sine
 
 
-def project_kernel(rope_heads, group, slice_rows, place, x_ref, own_ref, rest_ref, cos_ref, sin_ref, out_ref, w_ref):
-    @pl.when(pl.program_id(0) == 0)
-    def _():
-        lines = own_ref.shape[0] // slice_rows
-        mine = place[0]
-        for line in range(lines):
-            at = pl.multiple_of((line * group + mine) * slice_rows, slice_rows)
-            w_ref[pl.ds(at, slice_rows), :] = own_ref[line * slice_rows : (line + 1) * slice_rows, :]
-            for step in range(1, group):
-                at = pl.multiple_of((line * group + (mine ^ step)) * slice_rows, slice_rows)
-                first = (line * (group - 1) + step - 1) * slice_rows
-                w_ref[pl.ds(at, slice_rows), :] = rest_ref[first : first + slice_rows, :]
-
-    total = jnp.dot(x_ref[...], w_ref[...], preferred_element_type=jnp.float32)
-    cosine, sine = cos_ref[...], sin_ref[...]
-    for head in range(out_ref.shape[1] // HEAD_DIM):
-        columns = slice(head * HEAD_DIM, (head + 1) * HEAD_DIM)
-        part = total[:, columns]
-        if head < rope_heads:
-            part = rotated(part, cosine, sine)
-        out_ref[:, columns] = part.astype(out_ref.dtype)
-
-
-def project(place, tokens, own, rest, column_block, width, cosine, sine, rope_heads, group, slice_rows):
-    rows, depth = tokens.shape
-    tile = min(512, rows)
-    if rest is None:
-        rest = jnp.zeros((16, width), own.dtype)
-    kernel = functools.partial(project_kernel, rope_heads, group, slice_rows)
+def project_kernel(rope_heads, layout, place, *refs):
+    parts, weights = layout
+    inputs = len(parts) + len(weights)
+    x_refs, w_refs = refs[: len(parts)], refs[len(parts) : inputs]
+    cos_ref, sin_ref, out_ref, x_all, w_all, x_sems, w_sem = refs[inputs:]
+    slot = 0
+    w_copies, x_copies, rows_of = [], [], []
+    for ref, (column, pieces) in zip(w_refs, weights):
+        for source, rows, target in pieces:
+            at = pl.multiple_of(target(place), rows)
+            width = w_all.shape[1]
+            copy = pltpu.make_async_copy(
+                ref.at[pl.ds(source, rows), pl.ds(column, width)], w_all.at[pl.ds(at, rows), :], w_sem.at[slot]
+            )
+            copy.start()
+            w_copies.append(copy)
+            slot += 1
+    slot = 0
+    tile = x_all.shape[0]
+    for ref, targets in zip(x_refs, parts):
+        step = ref.shape[0] // len(targets)
+        for number, target in enumerate(targets):
+            copy = pltpu.make_async_copy(
+                ref.at[pl.ds(number * step, step), :], x_all.at[pl.ds(slot * step, step), :], x_sems.at[slot]
+            )
+            copy.start()
+            x_copies.append(copy)
+            rows_of.append(pl.multiple_of(target(place), step))
+            slot += 1
+    for copy in w_copies:
+        copy.wait()
+    count = len(x_copies)
+    step = tile // count
+    pair = 2 if count % 2 == 0 else 1
+    for first in range(0, count, pair):
+        for number in range(first, first + pair):
+            x_copies[number].wait()
+        total = jnp.dot(
+            x_all[first * step : (first + pair) * step, :], w_all[...], preferred_element_type=jnp.float32
+        )
+        for number in range(pair):
+            rows = pl.ds(rows_of[first + number], step)
+            cosine, sine = cos_ref[rows, :], sin_ref[rows, :]
+            for head in range(out_ref.shape[1] // HEAD_DIM):
+                columns = slice(head * HEAD_DIM, (head + 1) * HEAD_DIM)
+                part = total[number * step : (number + 1) * step, columns]
+                if head < rope_heads:
+                    part = rotated(part, cosine, sine)
+                out_ref[rows, columns] = part.astype(out_ref.dtype)
+
+
+def project(place, tokens, weights, width, cosine, sine, rope_heads):
+    rows = sum(part.shape[0] for part, _ in tokens)
+    depth = tokens[0][0].shape[1]
+    layout = ([targets for _, targets in tokens], [(column, pieces) for _, column, pieces in weights])
+    arrays = [part for part, _ in tokens] + [part for part, _, _ in weights]
+    dtype = tokens[0][0].dtype
     return pl.pallas_call(
-        kernel,
+        functools.partial(project_kernel, rope_heads, layout),
         out_shape=jax.ShapeDtypeStruct((rows, width), jnp.bfloat16),
-        grid_spec=pltpu.PrefetchScalarGridSpec(
-            num_scalar_prefetch=1,
-            grid=(rows // tile,),
-            in_specs=[
-                pl.BlockSpec((tile, depth), lambda i, s: (i, 0)),
-                pl.BlockSpec((own.shape[0], width), lambda i, s: (0, column_block)),
-                pl.BlockSpec(rest.shape, lambda i, s: (0, 0)),
-                pl.BlockSpec((tile, HEAD_DIM), lambda i, s: (i, 0)),
-                pl.BlockSpec((tile, HEAD_DIM), lambda i, s: (i, 0)),
-            ],
-            out_specs=pl.BlockSpec((tile, width), lambda i, s: (i, 0)),
-            scratch_shapes=[pltpu.VMEM((depth, width), own.dtype)],
-        ),
+        in_specs=[pl.BlockSpec(memory_space=pltpu.SMEM)]
+        + [pl.BlockSpec(memory_space=pl.ANY)] * len(arrays)
+        + [pl.BlockSpec(memory_space=pltpu.VMEM)] * 2,
+        out_specs=pl.BlockSpec(memory_space=pltpu.VMEM),
+        scratch_shapes=[
+            pltpu.VMEM((rows, depth), dtype),
+            pltpu.VMEM((depth, width), dtype),
+            pltpu.SemaphoreType.DMA((sum(len(targets) for _, targets in tokens),)),
+            pltpu.SemaphoreType.DMA((sum(len(pieces) for _, _, pieces in weights),)),
+        ],
         compiler_params=pltpu.CompilerParams(vmem_limit_bytes=VMEM_BYTES),
         cost_estimate=pl.CostEstimate(
             flops=2 * rows * depth * width, bytes_accessed=2 * depth * (rows + width), transcendentals=0
         ),
-    )(place, tokens, own, rest, cosine, sine)
+    )(place, *arrays, cosine, sine)
 
 
 def attend_kernel(kv_heads, share, halo_rows, bounds, q_ref, start_ref, halo_ref, kv_ref, out_ref, kv_all, sums, totals):
@@ -217,15 +242,54 @@
         lanes = [[place + group * i for i in range(lines)] for place in range(group)]
         return lax.all_gather(block, "ca", axis=0, tiled=True, axis_index_groups=lanes)
 
+    def ring(block):
+        held = [block]
+        for hop in range(1, lines):
+            held.append(lax.ppermute(held[-1], "ca", [(i, (i + group) % (group * lines)) for i in devices]))
+        return held
+
+    def gathered(array, column, members):
+        if group == 1:
+            return (array, column, [(0, array.shape[0], lambda s: 0)])
+        pieces = []
+        for at in range(lines):
+            for number, step in enumerate(members):
+                source = (at * len(members) + number) * slice_rows
+                pieces.append((source, slice_rows, lambda s, at=at, step=step: (at * group + (s[0] ^ step)) * slice_rows))
+        return (array, column, pieces)
+
+    def from_ring(held, members):
+        entries = []
+        for back, array in enumerate(held):
+            pieces = []
+            for number, step in enumerate(members):
+
+                def target(s, back=back, step=step):
+                    at = lax.rem(s[1] - back + lines, lines)
+                    return (at * group + (s[0] ^ step)) * slice_rows
+
+                pieces.append((number * slice_rows, slice_rows, target))
+            entries.append((array, 0, pieces))
+        return entries
+
     own_slices = along_lines(slice_for(mine))
-    rest_kv = rest_q = None
-    all_tokens = tokens
+    half = row_count // cores if group > 1 else row_count
+    token_parts = [
+        (tokens, [lambda s, i=i: s[0] * row_count + i * half for i in range(row_count // half)]),
+    ]
     if group > 1:
-        arrived = [to_partner(slice_for(mine ^ step), step) for step in range(1, group)]
-        rest_kv = along_lines(jnp.concatenate([a[:, q_width:] for a in arrived]))
-        rest_q = along_lines(jnp.concatenate([a[:, :q_width] for a in arrived]))
-
-        half = row_count // cores
+        others = range(1, group)
+        arrived = [to_partner(slice_for(mine ^ step), step) for step in others]
+        split = q_width // 2
+        rest_kv = ring(jnp.concatenate([a[:, q_width:] for a in arrived]))
+        rest_first = along_lines(jnp.concatenate([a[:, :split] for a in arrived]))
+        rest_second = ring(jnp.concatenate([a[:, split:q_width] for a in arrived]))
+        kv_weights = [gathered(own_slices, q_width, [0])] + from_ring(rest_kv, others)
+        q_weights = [
+            [gathered(own_slices, 0, [0]), gathered(rest_first, 0, others)],
+            [gathered(own_slices, split, [0])] + from_ring(rest_second, others),
+        ]
+
         both = ("ca", "tp")
 
         def cross(block, steps):
@@ -239,29 +303,25 @@
         near = cross(own_half, (1, 2))
         other = cross(own_half, (2, 1))
         far = cross(near, (2, 1))
-        all_tokens = jnp.zeros((group_rows, depth), tokens.dtype)
-        all_tokens = lax.dynamic_update_slice_in_dim(all_tokens, tokens, mine * row_count, 0)
         for block, steps in ((near, (1, 2)), (other, (2, 1)), (far, (3, 3))):
-            mate = swap(block)
-            step_here = jnp.where(core == 0, steps[0], steps[1])
-            step_mate = jnp.where(core == 0, steps[1], steps[0])
-            all_tokens = lax.dynamic_update_slice_in_dim(
-                all_tokens, block, (mine ^ step_here) * row_count + core * half, 0
-            )
-            all_tokens = lax.dynamic_update_slice_in_dim(
-                all_tokens, mate, (mine ^ step_mate) * row_count + (1 - core) * half, 0
-            )
+
+            def here(s, steps=steps):
+                return (s[0] ^ jnp.where(s[2] == 0, steps[0], steps[1])) * row_count + s[2] * half
+
+            def mate(s, steps=steps):
+                return (s[0] ^ jnp.where(s[2] == 0, steps[1], steps[0])) * row_count + (1 - s[2]) * half
+
+            token_parts += [(block, [here]), (swap(block), [mate])]
+    else:
+        split = q_width
+        kv_weights = [gathered(own_slices, q_width, [0])]
+        q_weights = [[gathered(own_slices, 0, [0])]]
 
     row_ids = line * group_rows + jnp.arange(group_rows, dtype=jnp.int32)
     starts = doc_starts(lengths, row_ids)
     cosine, sine = rope_tables(row_ids - starts)
-    place = mine.reshape(1).astype(jnp.int32)
-    kv = project(
-        place, all_tokens, own_slices, rest_kv, q_width // kv_width, kv_width, cosine, sine, kv_heads, group, slice_rows
-    )
-    query = project(
-        place, all_tokens, own_slices, rest_q, 0, q_width, cosine, sine, q_width // HEAD_DIM, group, slice_rows
-    )
+    place = jnp.stack([mine, line, core]).astype(jnp.int32)
+    kv = project(place, token_parts, kv_weights, kv_width, cosine, sine, kv_heads)
 
     halo_rows = REACH * row_count
     hops = -(-halo_rows // group_rows)
@@ -275,20 +335,22 @@
 
     window_starts = starts - (line * group_rows - halo_rows)
     result = jnp.zeros((row_count, w_query.shape[1]), jnp.bfloat16)
-    for step in reversed(range(group)):
-        part = attend(mine ^ step, row_count, query, window_starts, halo, kv, kv_heads)
-        if step > 0:
-            part = to_partner(part, step)
-        elif group == 1:
-            return part
-        result = lax.dynamic_update_slice_in_dim(result, part, (mine ^ step) * q_width, 1)
+    for number, weights in enumerate(q_weights):
+        query = project(place, token_parts, weights, split, cosine, sine, split // HEAD_DIM)
+        for step in reversed(range(group)):
+            part = attend(mine ^ step, row_count, query, window_starts, halo, kv, kv_heads)
+            if step > 0:
+                part = to_partner(part, step)
+            elif group == 1:
+                return part
+            result = lax.dynamic_update_slice_in_dim(result, part, (mine ^ step) * q_width + number * split, 1)
     return result
 
 
 def solution(mesh):
     size, cores = mesh.shape["ca"], mesh.shape["tp"]
     local_kv = KV_HEADS // cores
-    group = 4 if cores == 2 and local_kv % 4 == 0 and size % 4 == 0 else 1
+    group = 4 if cores == 2 and local_kv == 4 and size % 4 == 0 else 1
     placed = (P("ca", None), P(), P("ca", "tp"), P("ca", "tp"), P("ca", "tp"))
     body = functools.partial(per_device, group, size // group, cores)
     return jax.shard_map(body, mesh=mesh, in_specs=placed, out_specs=P("ca", "tp"), check_vma=False)

time: 230 us -> 311 us (1.35)
  Pallas kernels: 58.7 us -> 100 us
  starting transfers between devices: 11.8 us -> 40.7 us
  waiting for transfers between devices: 89.5 us -> 111 us
  local copies, waits for them, and re-layouts: 44.4 us -> 23.9 us
  other arithmetic: 7.42 us -> 19.5 us
    ppermute x0 -> x6, waiting for transfers between devices: none -> 36.3 us  [ring(): lax.ppermute(held[-1], 'ca', [(i, (i + group) % (group * lines)) for i in...]
    pallas_call x2 -> x3, Pallas kernels: 23 us -> 49.8 us  [project(): pl.pallas_call(functools.partial(project_kernel, rope_heads, layout), out...]
    all_gather x3 -> x2, waiting for transfers between devices: 26.1 us -> 0.01 us  [along_lines(): lax.all_gather(block, 'ca', axis=0, tiled=True, axis_index_groups=lanes)]
    dynamic_update_slice x11 -> x8, local copies, waits for them, and re-layouts: 20.6 us -> 0.91 us  [per_device(): lax.dynamic_update_slice_in_dim(result, part, (mine ^ step) * q_width + n...]
    ppermute x0 -> x6, starting transfers between devices: none -> 18.8 us  [ring(): lax.ppermute(held[-1], 'ca', [(i, (i + group) % (group * lines)) for i in...]
    ppermute x3, waiting for transfers between devices: 44.2 us -> 59.2 us  [cross(): return lax.ppermute(block, both, pairs)]
    pallas_call x4 -> x8, Pallas kernels: 35.6 us -> 50.3 us  [attend(): pl.pallas_call(kernel, out_shape=jax.ShapeDtypeStruct((chunk_rows, width)...]
    ppermute x6 -> x9, starting transfers between devices: 3.9 us -> 12.9 us  [to_partner(): return lax.ppermute(block, 'ca', [(i, i ^ step) for i in devices])]
  transfers between devices with their start and end apart: 16 -> 24, of which waited for: 7 -> 9; matrix products, arithmetic and copies ran while one was open for 20% -> 9% of each run, Pallas kernels for 22% -> 30%
where the time goes in v1:
time: 311 us; the launch traced here: 309 us
  waiting for transfers between devices  111 us (36%)
  Pallas kernels  100 us (32%)
  starting transfers between devices  40.7 us (13%)
  local copies, waits for them, and re-layouts  23.9 us (8%)
  other arithmetic  19.5 us (6%)
  between operations  13.9 us (4%)
    ppermute x3, waiting for transfers between devices, cross(): return lax.ppermute(block, both, pairs)  59.2 us
    pallas_call x8, Pallas kernels, attend(): pl.pallas_call(kernel, out_shape=jax.ShapeDtypeStruct((chunk_rows, width)...  50.3 us
    pallas_call x3, Pallas kernels, project(): pl.pallas_call(functools.partial(project_kernel, rope_heads, layout), out...  49.8 us
    ppermute x6, waiting for transfers between devices, ring(): lax.ppermute(held[-1], 'ca', [(i, (i + group) % (group * lines)) for i in...  36.3 us
    ppermute x6, starting transfers between devices, ring(): lax.ppermute(held[-1], 'ca', [(i, (i + group) % (group * lines)) for i in...  18.8 us
    ppermute x9, waiting for transfers between devices, to_partner(): return lax.ppermute(block, 'ca', [(i, i ^ step) for i in devices])  15.2 us
    ppermute x9, starting transfers between devices, to_partner(): return lax.ppermute(block, 'ca', [(i, i ^ step) for i in devices])  12.9 us
    unnamed x48, local copies, waits for them, and re-layouts  12 us
  transfers between devices with their start and end apart: 24, of which 9 were waited for; matrix products, arithmetic and copies ran while one was open for 9% of the time, Pallas kernels for 30%

profile of v1, /device:TPU:10, one launch (start us, length us, event | category | flops | bytes accessed | tf_op | source)
XLA Modules:
  0.0 308.9 jit_solution(12085261279581547660)
XLA Ops:
  6.5 1.9 constant_dynamic-slice_fusion.12
  13.8 2.4 collective-permute-start.8
  18.7 38.3 %collective-permute-done.refs_1_ = bf16[256,4096]{1,0:T(8,128)(2,1)} collective-permute-done((bf16[256,4096]{1,0:T(8,128)(2,1)S(1)}, bf16[256,4096]{1,0:T(8,128)(2,1)}, u32[]{:S(2)}, u32[]{:S(2)}) %collective-permute-start) | collective-permute-done | bytes 2097184 | tf_op jit(solution)/shard_map/ppermute | solution.py:297
  64.5 8.3 %collective-permute-done.7 = bf16[256,768]{1,0:T(8,128)(2,1)} collective-permute-done((bf16[256,768]{1,0:T(8,128)(2,1)}, bf16[256,768]{1,0:T(8,128)(2,1)}, u32[]{:S(2)}, u32[]{:S(2)}) %collective-permute-start.7) | collective-permute-done | bytes 393248 | tf_op jit(solution)/shard_map/ppermute | solution.py:239
  74.5 20.8 %collective-permute-done.4.refs_5_ = bf16[256,4096]{1,0:T(8,128)(2,1)} collective-permute-done((bf16[256,4096]{1,0:T(8,128)(2,1)}, bf16[256,4096]{1,0:T(8,128)(2,1)}, u32[]{:S(2)}, u32[]{:S(2)}) %collective-permute-start.4) | collective-permute-done | bytes 2097184 | tf_op jit(solution)/shard_map/ppermute | solution.py:297
  100.1 1.6 collective-permute-start.16
  102.5 8.9 %collective-permute-done.9.refs_9_ = bf16[768,256]{1,0:T(8,128)(2,1)S(1)} collective-permute-done((bf16[768,256]{1,0:T(8,128)(2,1)S(1)}, bf16[768,256]{1,0:T(8,128)(2,1)S(1)}, u32[]{:S(2)}, u32[]{:S(2)}) %collective-permute-start.9) | collective-permute-done | bytes 393248 | tf_op jit(solution)/shard_map/ppermute | solution.py:248
  111.4 3.6 %collective-permute-start.10 = (bf16[768,256]{1,0:T(8,128)(2,1)S(1)}, bf16[768,256]{1,0:T(8,128)(2,1)S(1)}, u32[]{:S(2)}, u32[]{:S(2)}) collective-permute-start(bf16[768,256]{1,0:T(8,128)(2,1)S(1)} %collective-permute-done.9.refs_9_), channel_id=1, source_target_pairs={{0,8},{2,10},{4,12},{6,14},{8,16},{10,18},{12,20},{14,22},{16,24},... | collective-permute-start | bytes 1179656 | tf_op jit(solution)/shard_map/ppermute | solution.py:248
  115.0 6.4 %fusion = (f32[2048,64]{1,0:T(8,128)}, f32[2048,64]{1,0:T(8,128)}, f32[2048,64]{1,0:T(8,128)}) fusion(f32[64]{0:T(128)} %multiply_power_fusion, f32[2048]{0:T(1024)} %get-tuple-element.29), kind=kLoop, calls=%fused_computation.19 | loop fusion | flops 262144 | bytes 1581312 | tf_op jit(solution)/shard_map/neg | solution.py:32
  121.4 11.9 %collective-permute-done.16.refs_9_ = bf16[768,256]{1,0:T(8,128)(2,1)S(1)} collective-permute-done((bf16[768,256]{1,0:T(8,128)(2,1)S(1)}, bf16[768,256]{1,0:T(8,128)(2,1)S(1)}, u32[]{:S(2)}, u32[]{:S(2)}) %collective-permute-start.16) | collective-permute-done | bytes 393248 | tf_op jit(solution)/shard_map/ppermute | solution.py:248
  133.3 6.1 %collective-permute-start.17 = (bf16[768,256]{1,0:T(8,128)(2,1)S(1)}, bf16[768,256]{1,0:T(8,128)(2,1)}, u32[]{:S(2)}, u32[]{:S(2)}) collective-permute-start(bf16[768,256]{1,0:T(8,128)(2,1)S(1)} %collective-permute-done.16.refs_9_), channel_id=1, source_target_pairs={{0,8},{2,10},{4,12},{6,14},{8,16},{10,18},{12,20},{14,22},{16,24},... | collective-permute-start | bytes 1179656 | tf_op jit(solution)/shard_map/ppermute | solution.py:248
  139.4 9.0 %collective-permute-done.10.refs_10_ = bf16[768,256]{1,0:T(8,128)(2,1)S(1)} collective-permute-done((bf16[768,256]{1,0:T(8,128)(2,1)S(1)}, bf16[768,256]{1,0:T(8,128)(2,1)S(1)}, u32[]{:S(2)}, u32[]{:S(2)}) %collective-permute-start.10) | collective-permute-done | bytes 393248 | tf_op jit(solution)/shard_map/ppermute | solution.py:248
  148.5 3.6 %collective-permute-start.11 = (bf16[768,256]{1,0:T(8,128)(2,1)S(1)}, bf16[768,256]{1,0:T(8,128)(2,1)}, u32[]{:S(2)}, u32[]{:S(2)}) collective-permute-start(bf16[768,256]{1,0:T(8,128)(2,1)S(1)} %collective-permute-done.10.refs_10_), channel_id=1, source_target_pairs={{0,8},{2,10},{4,12},{6,14},{8,16},{10,18},{12,20},{14,22},{16,24},... | collective-permute-start | bytes 1179656 | tf_op jit(solution)/shard_map/ppermute | solution.py:248
  155.9 3.7 %pad_maximum_fusion = (f32[2048,128]{1,0:T(8,128)S(1)}, f32[2048,128]{1,0:T(8,128)}) fusion(f32[2048,64]{1,0:T(8,128)} %get-tuple-element.28, f32[2048,64]{1,0:T(8,128)} %get-tuple-element.27, f32[2048,64]{1,0:T(8,128)} %get-tuple-element.26), kind=kLoop, calls=%fused_computation.10 | loop fusion | flops 524288 | bytes 3670016 | tf_op jit(solution)/shard_map/concatenate | solution.py:32
  159.9 2.3 collective-permute-start.18
  162.2 6.2 %collective-permute-done.11.refs_11_ = bf16[768,256]{1,0:T(8,128)(2,1)} collective-permute-done((bf16[768,256]{1,0:T(8,128)(2,1)S(1)}, bf16[768,256]{1,0:T(8,128)(2,1)}, u32[]{:S(2)}, u32[]{:S(2)}) %collective-permute-start.11) | collective-permute-done | bytes 393248 | tf_op jit(solution)/shard_map/ppermute | solution.py:248
  172.3 17.1 %shard_map.56.kv_ref = bf16[2048,256]{1,0:T(8,128)(2,1)S(1)} custom-call(s32[3]{0:T(128)S(1)} %copy-done.17, bf16[512,4096]{1,0:T(8,128)(2,1)} %refs_0_.5, bf16[256,4096]{1,0:T(8,128)(2,1)} %collective-permute-done.refs_1_, bf16[256,4096]{1,0:T(8,128)(2,1)} %collective-permute-done.1.refs_2_, bf16[256,4096]{1,0:T(8,128)(2,1)} %collective-permute-done.2.refs_3_, ...), custom_call_target="tpu_custom_call" | custom-call | flops 4294967296 | bytes 18874368 | tf_op jit(solution)/shard_map/pallas_call | solution.py:96
  190.4 3.7 %collective-permute-start.12 = (bf16[1536,256]{1,0:T(8,128)(2,1)}, bf16[1536,256]{1,0:T(8,128)(2,1)S(1)}, u32[]{:S(2)}, u32[]{:S(2)}) collective-permute-start(bf16[1536,256]{1,0:T(8,128)(2,1)} %slice.62), channel_id=1, source_target_pairs={{0,8},{2,10},{4,12},{6,14},{8,16},{10,18},{12,20},{14,22},{16,24},... | collective-permute-start | bytes 2359304 | tf_op jit(solution)/shard_map/ppermute | solution.py:332
  195.3 16.7 %shard_map.61.q_ref = bf16[2048,256]{1,0:T(8,128)(2,1)S(1)} custom-call(s32[3]{0:T(128)S(1)} %copy-done.17, bf16[512,4096]{1,0:T(8,128)(2,1)} %refs_0_.5, bf16[256,4096]{1,0:T(8,128)(2,1)} %collective-permute-done.refs_1_, bf16[256,4096]{1,0:T(8,128)(2,1)} %collective-permute-done.1.refs_2_, bf16[256,4096]{1,0:T(8,128)(2,1)} %collective-permute-done.2.refs_3_, ...), custom_call_target="tpu_custom_call" | custom-call | flops 4294967296 | bytes 18874368 | tf_op jit(solution)/shard_map/pallas_call | solution.py:96
  216.9 15.9 %shard_map.55.q_ref = bf16[2048,256]{1,0:T(8,128)(2,1)S(1)} custom-call(s32[3]{0:T(128)S(1)} %copy-done.18, bf16[512,4096]{1,0:T(8,128)(2,1)} %refs_0_.5, bf16[256,4096]{1,0:T(8,128)(2,1)} %collective-permute-done.refs_1_, bf16[256,4096]{1,0:T(8,128)(2,1)} %collective-permute-done.1.refs_2_, bf16[256,4096]{1,0:T(8,128)(2,1)} %collective-permute-done.2.refs_3_, ...), custom_call_target="tpu_custom_call" | custom-call | flops 4294967296 | bytes 18874368 | tf_op jit(solution)/shard_map/pallas_call | solution.py:96
  232.8 6.2 %shard_map.64 = bf16[512,256]{1,0:T(8,128)(2,1)S(1)} custom-call(s32[3,2]{1,0:T(4,128)S(1)} %pad_add_fusion.2.bounds, bf16[2048,256]{1,0:T(8,128)(2,1)S(1)} %copy-done.1, s32[2048,1]{1,0:T(8,128)S(1)} %copy.14.start_ref, bf16[1536,256]{1,0:T(8,128)(2,1)S(1)} %collective-permute-done.12.halo_ref, bf16[2048,256]{1,0:T(8,128)(2,1)S(1)} %shard_map.56.kv_ref), custom_call_target="tpu_custom_call" | custom-call | flops 536870912 | bytes 524288 | tf_op jit(solution)/shard_map/pallas_call | solution.py:187
  239.1 2.9 collective-permute-start.21
  242.0 4.0 %shard_map.57 = bf16[512,256]{1,0:T(8,128)(2,1)S(1)} custom-call(s32[3,2]{1,0:T(4,128)S(1)} %get-tuple-element.31.bounds, bf16[2048,256]{1,0:T(8,128)(2,1)S(1)} %shard_map.55.q_ref, s32[2048,1]{1,0:T(8,128)S(1)} %copy.14.start_ref, bf16[1536,256]{1,0:T(8,128)(2,1)S(1)} %collective-permute-done.12.halo_ref, bf16[2048,256]{1,0:T(8,128)(2,1)S(1)} %shard_map.56.kv_ref), custom_call_target="tpu_custom_call" | custom-call | flops 536870912 | bytes 524288 | tf_op jit(solution)/shard_map/pallas_call | solution.py:187
  246.0 2.4 collective-permute-start.13
  248.4 6.5 %shard_map.63 = bf16[512,256]{1,0:T(8,128)(2,1)S(1)} custom-call(s32[3,2]{1,0:T(4,128)S(1)} %get-tuple-element.32.bounds, bf16[2048,256]{1,0:T(8,128)(2,1)S(1)} %copy-done.1, s32[2048,1]{1,0:T(8,128)S(1)} %copy.14.start_ref, bf16[1536,256]{1,0:T(8,128)(2,1)S(1)} %collective-permute-done.12.halo_ref, bf16[2048,256]{1,0:T(8,128)(2,1)S(1)} %shard_map.56.kv_ref), custom_call_target="tpu_custom_call" | custom-call | flops 536870912 | bytes 524288 | tf_op jit(solution)/shard_map/pallas_call | solution.py:187
  254.9 3.8 %collective-permute-start.20 = (bf16[512,256]{1,0:T(8,128)(2,1)S(1)}, bf16[512,256]{1,0:T(8,128)(2,1)S(1)}, u32[]{:S(2)}, u32[]{:S(2)}) collective-permute-start(bf16[512,256]{1,0:T(8,128)(2,1)S(1)} %shard_map.63), channel_id=1, source_target_pairs={{0,4},{2,6},{4,0},{6,2},{8,12},{10,14},{12,8},{14,10},{16,20},{18,... | collective-permute-start | bytes 786440 | tf_op jit(solution)/shard_map/ppermute | solution.py:239
  258.7 6.2 %shard_map.59 = bf16[512,256]{1,0:T(8,128)(2,1)S(1)} custom-call(s32[3,2]{1,0:T(4,128)S(1)} %pad_add_fusion.2.bounds, bf16[2048,256]{1,0:T(8,128)(2,1)S(1)} %shard_map.55.q_ref, s32[2048,1]{1,0:T(8,128)S(1)} %copy.14.start_ref, bf16[1536,256]{1,0:T(8,128)(2,1)S(1)} %collective-permute-done.12.halo_ref, bf16[2048,256]{1,0:T(8,128)(2,1)S(1)} %shard_map.56.kv_ref), custom_call_target="tpu_custom_call" | custom-call | flops 536870912 | bytes 524288 | tf_op jit(solution)/shard_map/pallas_call | solution.py:187
  265.0 6.3 %shard_map.58 = bf16[512,256]{1,0:T(8,128)(2,1)S(1)} custom-call(s32[3,2]{1,0:T(4,128)S(1)} %get-tuple-element.32.bounds, bf16[2048,256]{1,0:T(8,128)(2,1)S(1)} %shard_map.55.q_ref, s32[2048,1]{1,0:T(8,128)S(1)} %copy.14.start_ref, bf16[1536,256]{1,0:T(8,128)(2,1)S(1)} %collective-permute-done.12.halo_ref, bf16[2048,256]{1,0:T(8,128)(2,1)S(1)} %shard_map.56.kv_ref), custom_call_target="tpu_custom_call" | custom-call | flops 536870912 | bytes 524288 | tf_op jit(solution)/shard_map/pallas_call | solution.py:187
  271.4 4.0 %shard_map.62 = bf16[512,256]{1,0:T(8,128)(2,1)S(1)} custom-call(s32[3,2]{1,0:T(4,128)S(1)} %get-tuple-element.31.bounds, bf16[2048,256]{1,0:T(8,128)(2,1)S(1)} %copy-done.1, s32[2048,1]{1,0:T(8,128)S(1)} %copy.14.start_ref, bf16[1536,256]{1,0:T(8,128)(2,1)S(1)} %collective-permute-done.12.halo_ref, bf16[2048,256]{1,0:T(8,128)(2,1)S(1)} %shard_map.56.kv_ref), custom_call_target="tpu_custom_call" | custom-call | flops 536870912 | bytes 524288 | tf_op jit(solution)/shard_map/pallas_call | solution.py:187
  275.4 8.6 %shard_map.65 = bf16[512,256]{1,0:T(8,128)(2,1)S(1)} custom-call(s32[3,2]{1,0:T(4,128)S(1)} %pad_add_fusion.3.bounds, bf16[2048,256]{1,0:T(8,128)(2,1)S(1)} %copy-done.1, s32[2048,1]{1,0:T(8,128)S(1)} %copy.14.start_ref, bf16[1536,256]{1,0:T(8,128)(2,1)S(1)} %collective-permute-done.12.halo_ref, bf16[2048,256]{1,0:T(8,128)(2,1)S(1)} %shard_map.56.kv_ref), custom_call_target="tpu_custom_call" | custom-call | flops 536870912 | bytes 524288 | tf_op jit(solution)/shard_map/pallas_call | solution.py:187
  284.0 8.6 %shard_map.60 = bf16[512,256]{1,0:T(8,128)(2,1)S(1)} custom-call(s32[3,2]{1,0:T(4,128)S(1)} %pad_add_fusion.3.bounds, bf16[2048,256]{1,0:T(8,128)(2,1)S(1)} %shard_map.55.q_ref, s32[2048,1]{1,0:T(8,128)S(1)} %copy.14.start_ref, bf16[1536,256]{1,0:T(8,128)(2,1)S(1)} %collective-permute-done.12.halo_ref, bf16[2048,256]{1,0:T(8,128)(2,1)S(1)} %shard_map.56.kv_ref), custom_call_target="tpu_custom_call" | custom-call | flops 536870912 | bytes 524288 | tf_op jit(solution)/shard_map/pallas_call | solution.py:187
  293.1 6.8 %collective-permute-done.19 = bf16[512,256]{1,0:T(8,128)(2,1)S(1)} collective-permute-done((bf16[512,256]{1,0:T(8,128)(2,1)S(1)}, bf16[512,256]{1,0:T(8,128)(2,1)S(1)}, u32[]{:S(2)}, u32[]{:S(2)}) %collective-permute-start.19) | collective-permute-done | bytes 262176 | tf_op jit(solution)/shard_map/ppermute | solution.py:239
  (138 shorter events, 40.1 us)
Async XLA Ops:
  6.5 161.8 %all-gather.3.cloned.1.call-start = ((), (), s32[]{:S(2)}) async-start(), calls=%async_computation | async-start | bytes 1966080 | tf_op jit(solution)/shard_map/all_gather | solution.py:243
  8.5 48.6 %collective-permute-start = (bf16[256,4096]{1,0:T(8,128)(2,1)S(1)}, bf16[256,4096]{1,0:T(8,128)(2,1)}, u32[]{:S(2)}, u32[]{:S(2)}) collective-permute-start(bf16[256,4096]{1,0:T(8,128)(2,1)S(1)} %constant_dynamic-slice_fusion.12), channel_id=1, source_target_pairs={{0,2},{1,5},{2,0},{3,7},{4,6},{5,1},{6,4},{7,3},{8,10},{9,13},{10,... | collective-permute-start | bytes 6291464 | tf_op jit(solution)/shard_map/ppermute | solution.py:297
  9.1 64.9 %collective-permute-start.2 = (bf16[256,4096]{1,0:T(8,128)(2,1)S(1)}, bf16[256,4096]{1,0:T(8,128)(2,1)}, u32[]{:S(2)}, u32[]{:S(2)}) collective-permute-start(bf16[256,4096]{1,0:T(8,128)(2,1)S(1)} %constant_dynamic-slice_fusion.12), channel_id=1, source_target_pairs={{0,4},{1,3},{2,6},{3,1},{4,0},{5,7},{6,2},{7,5},{8,12},{9,11},{10,... | collective-permute-start | bytes 6291464 | tf_op jit(solution)/shard_map/ppermute | solution.py:297
  12.5 60.3 %collective-permute-start.7 = (bf16[256,768]{1,0:T(8,128)(2,1)}, bf16[256,768]{1,0:T(8,128)(2,1)}, u32[]{:S(2)}, u32[]{:S(2)}) collective-permute-start(bf16[256,768]{1,0:T(8,128)(2,1)} %pad_maximum_fusion.4), channel_id=1, source_target_pairs={{0,4},{2,6},{4,0},{6,2},{8,12},{10,14},{12,8},{14,10},{16,20},{18,... | collective-permute-start | bytes 1179656 | tf_op jit(solution)/shard_map/ppermute | solution.py:239
  13.8 82.5 %collective-permute-start.8 = (bf16[256,768]{1,0:T(8,128)(2,1)}, bf16[256,768]{1,0:T(8,128)(2,1)S(1)}, u32[]{:S(2)}, u32[]{:S(2)}) collective-permute-start(bf16[256,768]{1,0:T(8,128)(2,1)} %pad_maximum_fusion.5), channel_id=1, source_target_pairs={{0,6},{2,4},{4,2},{6,0},{8,14},{10,12},{12,10},{14,8},{16,22},{18,... | collective-permute-start | bytes 1179656 | tf_op jit(solution)/shard_map/ppermute | solution.py:239
  16.3 80.1 %collective-permute-start.6 = (bf16[256,768]{1,0:T(8,128)(2,1)S(1)}, bf16[256,768]{1,0:T(8,128)(2,1)S(1)}, u32[]{:S(2)}, u32[]{:S(2)}) collective-permute-start(bf16[256,768]{1,0:T(8,128)(2,1)S(1)} %pad_maximum_fusion.3), channel_id=1, source_target_pairs={{0,2},{2,0},{4,6},{6,4},{8,10},{10,8},{12,14},{14,12},{16,18},{18,... | collective-permute-start | bytes 1179656 | tf_op jit(solution)/shard_map/ppermute | solution.py:239
  17.7 195.3 %all-gather.5.cloned.1.call-start = ((), (), s32[]{:S(2)}) async-start(), calls=%async_computation.1 | async-start | bytes 1966080 | tf_op jit(solution)/shard_map/all_gather | solution.py:243
  57.0 38.3 %collective-permute-start.4 = (bf16[256,4096]{1,0:T(8,128)(2,1)}, bf16[256,4096]{1,0:T(8,128)(2,1)}, u32[]{:S(2)}, u32[]{:S(2)}) collective-permute-start(bf16[256,4096]{1,0:T(8,128)(2,1)} %collective-permute-done.refs_1_), channel_id=1, source_target_pairs={{0,4},{1,3},{2,6},{3,1},{4,0},{5,7},{6,2},{7,5},{8,12},{9,11},{10,... | collective-permute-start | bytes 6291464 | tf_op jit(solution)/shard_map/ppermute | solution.py:297
  73.9 94.5 %collective-permute-start.1 = (bf16[256,4096]{1,0:T(8,128)(2,1)}, bf16[256,4096]{1,0:T(8,128)(2,1)}, u32[]{:S(2)}, u32[]{:S(2)}) collective-permute-start(bf16[256,4096]{1,0:T(8,128)(2,1)} %collective-permute-done.refs_1_), channel_id=1, source_target_pairs={{0,1},{1,0},{2,3},{3,2},{4,5},{5,4},{6,7},{7,6},{8,9},{9,8},{10,11... | collective-permute-start | bytes 6291464 | tf_op jit(solution)/shard_map/ppermute | solution.py:300
  74.0 94.4 %collective-permute-start.3 = (bf16[256,4096]{1,0:T(8,128)(2,1)}, bf16[256,4096]{1,0:T(8,128)(2,1)}, u32[]{:S(2)}, u32[]{:S(2)}) collective-permute-start(bf16[256,4096]{1,0:T(8,128)(2,1)} %collective-permute-done.2.refs_3_), channel_id=1, source_target_pairs={{0,1},{1,0},{2,3},{3,2},{4,5},{5,4},{6,7},{7,6},{8,9},{9,8},{10,11... | collective-permute-start | bytes 6291464 | tf_op jit(solution)/shard_map/ppermute | solution.py:300
  95.3 73.1 %collective-permute-start.5 = (bf16[256,4096]{1,0:T(8,128)(2,1)}, bf16[256,4096]{1,0:T(8,128)(2,1)}, u32[]{:S(2)}, u32[]{:S(2)}) collective-permute-start(bf16[256,4096]{1,0:T(8,128)(2,1)} %collective-permute-done.4.refs_5_), channel_id=1, source_target_pairs={{0,1},{1,0},{2,3},{3,2},{4,5},{5,4},{6,7},{7,6},{8,9},{9,8},{10,11... | collective-permute-start | bytes 6291464 | tf_op jit(solution)/shard_map/ppermute | solution.py:300
  97.2 14.2 %collective-permute-start.9 = (bf16[768,256]{1,0:T(8,128)(2,1)S(1)}, bf16[768,256]{1,0:T(8,128)(2,1)S(1)}, u32[]{:S(2)}, u32[]{:S(2)}) collective-permute-start(bf16[768,256]{1,0:T(8,128)(2,1)S(1)} %pad_maximum_fusion.7.refs_8_), channel_id=1, source_target_pairs={{0,8},{2,10},{4,12},{6,14},{8,16},{10,18},{12,20},{14,22},{16,24},... | collective-permute-start | bytes 1179656 | tf_op jit(solution)/shard_map/ppermute | solution.py:248
  100.1 33.2 %collective-permute-start.16 = (bf16[768,256]{1,0:T(8,128)(2,1)S(1)}, bf16[768,256]{1,0:T(8,128)(2,1)S(1)}, u32[]{:S(2)}, u32[]{:S(2)}) collective-permute-start(bf16[768,256]{1,0:T(8,128)(2,1)S(1)} %pad_maximum_fusion.8.refs_8_), channel_id=1, source_target_pairs={{0,8},{2,10},{4,12},{6,14},{8,16},{10,18},{12,20},{14,22},{16,24},... | collective-permute-start | bytes 1179656 | tf_op jit(solution)/shard_map/ppermute | solution.py:248
  111.4 21.9 %copy-start.11 = (bf16[768,256]{1,0:T(8,128)(2,1)}, bf16[768,256]{1,0:T(8,128)(2,1)S(1)}, u32[]{:S(2)}) copy-start(bf16[768,256]{1,0:T(8,128)(2,1)S(1)} %collective-permute-done.9.refs_9_) | copy-start | bytes 1179652
  111.4 37.1 %collective-permute-start.10 = (bf16[768,256]{1,0:T(8,128)(2,1)S(1)}, bf16[768,256]{1,0:T(8,128)(2,1)S(1)}, u32[]{:S(2)}, u32[]{:S(2)}) collective-permute-start(bf16[768,256]{1,0:T(8,128)(2,1)S(1)} %collective-permute-done.9.refs_9_), channel_id=1, source_target_pairs={{0,8},{2,10},{4,12},{6,14},{8,16},{10,18},{12,20},{14,22},{16,24},... | collective-permute-start | bytes 1179656 | tf_op jit(solution)/shard_map/ppermute | solution.py:248
  121.4 34.5 %copy-start.22 = (s32[1,2]{1,0:T(1,128)S(1)}, s32[1,2]{1,0:T(1,128)}, u32[]{:S(2)}) copy-start(s32[1,2]{1,0:T(1,128)} %fusion.15) | copy-start | bytes 28
  133.3 26.3 %copy-start.13 = (bf16[768,256]{1,0:T(8,128)(2,1)}, bf16[768,256]{1,0:T(8,128)(2,1)S(1)}, u32[]{:S(2)}) copy-start(bf16[768,256]{1,0:T(8,128)(2,1)S(1)} %collective-permute-done.16.refs_9_) | copy-start | bytes 1179652
  133.3 26.6 %collective-permute-start.17 = (bf16[768,256]{1,0:T(8,128)(2,1)S(1)}, bf16[768,256]{1,0:T(8,128)(2,1)}, u32[]{:S(2)}, u32[]{:S(2)}) collective-permute-start(bf16[768,256]{1,0:T(8,128)(2,1)S(1)} %collective-permute-done.16.refs_9_), channel_id=1, source_target_pairs={{0,8},{2,10},{4,12},{6,14},{8,16},{10,18},{12,20},{14,22},{16,24},... | collective-permute-start | bytes 1179656 | tf_op jit(solution)/shard_map/ppermute | solution.py:248
  148.5 19.9 %collective-permute-start.11 = (bf16[768,256]{1,0:T(8,128)(2,1)S(1)}, bf16[768,256]{1,0:T(8,128)(2,1)}, u32[]{:S(2)}, u32[]{:S(2)}) collective-permute-start(bf16[768,256]{1,0:T(8,128)(2,1)S(1)} %collective-permute-done.10.refs_10_), channel_id=1, source_target_pairs={{0,8},{2,10},{4,12},{6,14},{8,16},{10,18},{12,20},{14,22},{16,24},... | collective-permute-start | bytes 1179656 | tf_op jit(solution)/shard_map/ppermute | solution.py:248
  159.6 29.8 %copy-start.2 = (f32[2048,128]{1,0:T(8,128)}, f32[2048,128]{1,0:T(8,128)S(1)}, u32[]{:S(2)}) copy-start(f32[2048,128]{1,0:T(8,128)S(1)} %get-tuple-element.41.refs_9_.refs_12_) | copy-start | bytes 3145732
  159.9 34.1 %collective-permute-start.18 = (bf16[768,256]{1,0:T(8,128)(2,1)}, bf16[768,256]{1,0:T(8,128)(2,1)}, u32[]{:S(2)}, u32[]{:S(2)}) collective-permute-start(bf16[768,256]{1,0:T(8,128)(2,1)} %collective-permute-done.17.refs_10_), channel_id=1, source_target_pairs={{0,8},{2,10},{4,12},{6,14},{8,16},{10,18},{12,20},{14,22},{16,24},... | collective-permute-start | bytes 1179656 | tf_op jit(solution)/shard_map/ppermute | solution.py:248
  172.3 21.8 %copy-start.10 = (bf16[768,256]{1,0:T(8,128)(2,1)S(1)}, bf16[768,256]{1,0:T(8,128)(2,1)}, u32[]{:S(2)}) copy-start(bf16[768,256]{1,0:T(8,128)(2,1)} %copy-done.9) | copy-start | bytes 1179652
  172.3 21.8 %copy-start.14 = (bf16[768,256]{1,0:T(8,128)(2,1)S(1)}, bf16[768,256]{1,0:T(8,128)(2,1)}, u32[]{:S(2)}) copy-start(bf16[768,256]{1,0:T(8,128)(2,1)} %copy-done.13) | copy-start | bytes 1179652
  189.4 23.6 %copy-start.18 = (s32[3]{0:T(128)S(1)}, s32[3]{0:T(128)}, u32[]{:S(2)}) copy-start(s32[3]{0:T(128)} %pad_add_fusion.4.place) | copy-start | bytes 40
  190.4 42.4 %collective-permute-start.12 = (bf16[1536,256]{1,0:T(8,128)(2,1)}, bf16[1536,256]{1,0:T(8,128)(2,1)S(1)}, u32[]{:S(2)}, u32[]{:S(2)}) collective-permute-start(bf16[1536,256]{1,0:T(8,128)(2,1)} %slice.62), channel_id=1, source_target_pairs={{0,8},{2,10},{4,12},{6,14},{8,16},{10,18},{12,20},{14,22},{16,24},... | collective-permute-start | bytes 2359304 | tf_op jit(solution)/shard_map/ppermute | solution.py:332
  216.9 15.9 %copy-start.1 = (bf16[2048,256]{1,0:T(8,128)(2,1)S(1)}, bf16[2048,256]{1,0:T(8,128)(2,1)}, u32[]{:S(2)}) copy-start(bf16[2048,256]{1,0:T(8,128)(2,1)} %copy-done) | copy-start | bytes 3145732
  239.1 60.9 %collective-permute-start.21 = (bf16[512,256]{1,0:T(8,128)(2,1)S(1)}, bf16[512,256]{1,0:T(8,128)(2,1)S(1)}, u32[]{:S(2)}, u32[]{:S(2)}) collective-permute-start(bf16[512,256]{1,0:T(8,128)(2,1)S(1)} %shard_map.64), channel_id=1, source_target_pairs={{0,2},{2,0},{4,6},{6,4},{8,10},{10,8},{12,14},{14,12},{16,18},{18,... | collective-permute-start | bytes 786440 | tf_op jit(solution)/shard_map/ppermute | solution.py:239
  246.0 46.5 %collective-permute-start.13 = (bf16[512,256]{1,0:T(8,128)(2,1)S(1)}, bf16[512,256]{1,0:T(8,128)(2,1)S(1)}, u32[]{:S(2)}, u32[]{:S(2)}) collective-permute-start(bf16[512,256]{1,0:T(8,128)(2,1)S(1)} %shard_map.57), channel_id=1, source_target_pairs={{0,6},{2,4},{4,2},{6,0},{8,14},{10,12},{12,10},{14,8},{16,22},{18,... | collective-permute-start | bytes 786440 | tf_op jit(solution)/shard_map/ppermute | solution.py:239
  254.9 45.0 %collective-permute-start.20 = (bf16[512,256]{1,0:T(8,128)(2,1)S(1)}, bf16[512,256]{1,0:T(8,128)(2,1)S(1)}, u32[]{:S(2)}, u32[]{:S(2)}) collective-permute-start(bf16[512,256]{1,0:T(8,128)(2,1)S(1)} %shard_map.63), channel_id=1, source_target_pairs={{0,4},{2,6},{4,0},{6,2},{8,12},{10,14},{12,8},{14,10},{16,20},{18,... | collective-permute-start | bytes 786440 | tf_op jit(solution)/shard_map/ppermute | solution.py:239
  264.9 28.0 %collective-permute-start.15 = (bf16[512,256]{1,0:T(8,128)(2,1)S(1)}, bf16[512,256]{1,0:T(8,128)(2,1)S(1)}, u32[]{:S(2)}, u32[]{:S(2)}) collective-permute-start(bf16[512,256]{1,0:T(8,128)(2,1)S(1)} %shard_map.59), channel_id=1, source_target_pairs={{0,2},{2,0},{4,6},{6,4},{8,10},{10,8},{12,14},{14,12},{16,18},{18,... | collective-permute-start | bytes 786440 | tf_op jit(solution)/shard_map/ppermute | solution.py:239
  271.3 21.6 %collective-permute-start.14 = (bf16[512,256]{1,0:T(8,128)(2,1)S(1)}, bf16[512,256]{1,0:T(8,128)(2,1)S(1)}, u32[]{:S(2)}, u32[]{:S(2)}) collective-permute-start(bf16[512,256]{1,0:T(8,128)(2,1)S(1)} %shard_map.58), channel_id=1, source_target_pairs={{0,4},{2,6},{4,0},{6,2},{8,12},{10,14},{12,8},{14,10},{16,20},{18,... | collective-permute-start | bytes 786440 | tf_op jit(solution)/shard_map/ppermute | solution.py:239
  292.6 7.3 %collective-permute-start.19 = (bf16[512,256]{1,0:T(8,128)(2,1)S(1)}, bf16[512,256]{1,0:T(8,128)(2,1)S(1)}, u32[]{:S(2)}, u32[]{:S(2)}) collective-permute-start(bf16[512,256]{1,0:T(8,128)(2,1)S(1)} %shard_map.62), channel_id=1, source_target_pairs={{0,6},{2,4},{4,2},{6,0},{8,14},{10,12},{12,10},{14,8},{16,22},{18,... | collective-permute-start | bytes 786440 | tf_op jit(solution)/shard_map/ppermute | solution.py:239
  (16 other events, 43.0 us)
Sparse Core Ops, SparseCore 0:
  17.8 36.2 all-gather.2
  97.3 60.7 all-gather.4

commit v2 on v1

--- a/solution.py
+++ b/solution.py
@@ -36,81 +36,78 @@
     return values * cosine + pltpu.roll(values, HEAD_DIM // 2, 1) * sine
 
 
-def project_kernel(rope_heads, layout, place, *refs):
+def project_kernel(rope_heads, layout, based, place, *refs):
     parts, weights = layout
-    inputs = len(parts) + len(weights)
-    x_refs, w_refs = refs[: len(parts)], refs[len(parts) : inputs]
-    cos_ref, sin_ref, out_ref, x_all, w_all, x_sems, w_sem = refs[inputs:]
+    x_refs, w_refs = refs[: len(parts)], refs[len(parts) : len(parts) + len(weights)]
+    refs = refs[len(parts) + len(weights) :]
+    if based:
+        base_ref, refs = refs[0], refs[1:]
+    cos_ref, sin_ref, out_ref, x_all, w_all, x_sems, w_sem = refs
+    width, depth = out_ref.shape[1], x_all.shape[2]
     slot = 0
-    w_copies, x_copies, rows_of = [], [], []
+    w_copies, x_copies = [], []
     for ref, (column, pieces) in zip(w_refs, weights):
         for source, rows, target in pieces:
             at = pl.multiple_of(target(place), rows)
-            width = w_all.shape[1]
             copy = pltpu.make_async_copy(
                 ref.at[pl.ds(source, rows), pl.ds(column, width)], w_all.at[pl.ds(at, rows), :], w_sem.at[slot]
             )
             copy.start()
             w_copies.append(copy)
             slot += 1
-    slot = 0
-    tile = x_all.shape[0]
+    slots, step = x_all.shape[0], x_all.shape[1]
     for ref, targets in zip(x_refs, parts):
-        step = ref.shape[0] // len(targets)
         for number, target in enumerate(targets):
-            copy = pltpu.make_async_copy(
-                ref.at[pl.ds(number * step, step), :], x_all.at[pl.ds(slot * step, step), :], x_sems.at[slot]
-            )
-            copy.start()
-            x_copies.append(copy)
-            rows_of.append(pl.multiple_of(target(place), step))
-            slot += 1
+            at = len(x_copies) % slots
+            copy = pltpu.make_async_copy(ref.at[pl.ds(number * step, step), :], x_all.at[at], x_sems.at[at])
+            x_copies.append((copy, pl.multiple_of(target(place), step), at))
+    for copy, _, _ in x_copies[: slots - 1]:
+        copy.start()
+    if based:
+        out_ref[...] = base_ref[...]
     for copy in w_copies:
         copy.wait()
-    count = len(x_copies)
-    step = tile // count
-    pair = 2 if count % 2 == 0 else 1
-    for first in range(0, count, pair):
-        for number in range(first, first + pair):
-            x_copies[number].wait()
-        total = jnp.dot(
-            x_all[first * step : (first + pair) * step, :], w_all[...], preferred_element_type=jnp.float32
-        )
-        for number in range(pair):
-            rows = pl.ds(rows_of[first + number], step)
-            cosine, sine = cos_ref[rows, :], sin_ref[rows, :]
-            for head in range(out_ref.shape[1] // HEAD_DIM):
-                columns = slice(head * HEAD_DIM, (head + 1) * HEAD_DIM)
-                part = total[number * step : (number + 1) * step, columns]
-                if head < rope_heads:
-                    part = rotated(part, cosine, sine)
-                out_ref[rows, columns] = part.astype(out_ref.dtype)
-
-
-def project(place, tokens, weights, width, cosine, sine, rope_heads):
-    rows = sum(part.shape[0] for part, _ in tokens)
-    depth = tokens[0][0].shape[1]
+    for number, (copy, at, slot) in enumerate(x_copies):
+        if number + slots - 1 < len(x_copies):
+            x_copies[number + slots - 1][0].start()
+        copy.wait()
+        total = jnp.dot(x_all[slot], w_all[...], preferred_element_type=jnp.float32)
+        rows = pl.ds(at, step)
+        cosine, sine = cos_ref[rows, :], sin_ref[rows, :]
+        for head in range(width // HEAD_DIM):
+            columns = slice(head * HEAD_DIM, (head + 1) * HEAD_DIM)
+            part = total[:, columns]
+            if head < rope_heads:
+                part = rotated(part, cosine, sine)
+            out_ref[rows, columns] = part.astype(out_ref.dtype)
+
+
+def project(place, tokens, weights, width, cosine, sine, rope_heads, base=None):
+    rows, depth = cosine.shape[0], tokens[0][0].shape[1]
+    step = tokens[0][0].shape[0] // len(tokens[0][1])
+    worked = sum(part.shape[0] for part, _ in tokens)
     layout = ([targets for _, targets in tokens], [(column, pieces) for _, column, pieces in weights])
     arrays = [part for part, _ in tokens] + [part for part, _, _ in weights]
     dtype = tokens[0][0].dtype
+    bases = [] if base is None else [base]
     return pl.pallas_call(
-        functools.partial(project_kernel, rope_heads, layout),
+        functools.partial(project_kernel, rope_heads, layout, base is not None),
         out_shape=jax.ShapeDtypeStruct((rows, width), jnp.bfloat16),
         in_specs=[pl.BlockSpec(memory_space=pltpu.SMEM)]
         + [pl.BlockSpec(memory_space=pl.ANY)] * len(arrays)
-        + [pl.BlockSpec(memory_space=pltpu.VMEM)] * 2,
+        + [pl.BlockSpec(memory_space=pltpu.VMEM)] * (2 + len(bases)),
         out_specs=pl.BlockSpec(memory_space=pltpu.VMEM),
         scratch_shapes=[
-            pltpu.VMEM((rows, depth), dtype),
+            pltpu.VMEM((4, step, depth), dtype),
             pltpu.VMEM((depth, width), dtype),
-            pltpu.SemaphoreType.DMA((sum(len(targets) for _, targets in tokens),)),
+            pltpu.SemaphoreType.DMA((4,)),
             pltpu.SemaphoreType.DMA((sum(len(pieces) for _, _, pieces in weights),)),
         ],
         compiler_params=pltpu.CompilerParams(vmem_limit_bytes=VMEM_BYTES),
         cost_estimate=pl.CostEstimate(
-            flops=2 * rows * depth * width, bytes_accessed=2 * depth * (rows + width), transcendentals=0
+            flops=worked * width, bytes_accessed=worked * width, transcendentals=0
         ),
-    )(place, *arrays, cosine, sine)
+    )(place, *arrays, *bases, cosine, sine)
 
 
 def attend_kernel(kv_heads, share, halo_rows, bounds, q_ref, start_ref, halo_ref, kv_ref, out_ref, kv_all, sums, totals):
@@ -242,11 +239,10 @@
         lanes = [[place + group * i for i in range(lines)] for place in range(group)]
         return lax.all_gather(block, "ca", axis=0, tiled=True, axis_index_groups=lanes)
 
-    def ring(block):
-        held = [block]
-        for hop in range(1, lines):
-            held.append(lax.ppermute(held[-1], "ca", [(i, (i + group) % (group * lines)) for i in devices]))
-        return held
+    def directly(block):
+        total = group * lines
+        shifts = [[(i, (i + group * back) % total) for i in devices] for back in range(1, lines)]
+        return [block] + [lax.ppermute(block, "ca", pairs) for pairs in shifts]
 
     def gathered(array, column, members):
         if group == 1:
@@ -258,7 +254,7 @@
                 pieces.append((source, slice_rows, lambda s, at=at, step=step: (at * group + (s[0] ^ step)) * slice_rows))
         return (array, column, pieces)
 
-    def from_ring(held, members):
+    def from_lines(held, members):
         entries = []
         for back, array in enumerate(held):
             pieces = []
@@ -281,13 +277,13 @@
         others = range(1, group)
         arrived = [to_partner(slice_for(mine ^ step), step) for step in others]
         split = q_width // 2
-        rest_kv = ring(jnp.concatenate([a[:, q_width:] for a in arrived]))
-        rest_first = along_lines(jnp.concatenate([a[:, :split] for a in arrived]))
-        rest_second = ring(jnp.concatenate([a[:, split:q_width] for a in arrived]))
-        kv_weights = [gathered(own_slices, q_width, [0])] + from_ring(rest_kv, others)
+        rest_kv = along_lines(jnp.concatenate([a[:, q_width:] for a in arrived]))
+        rest_first = directly(jnp.concatenate([a[:, :split] for a in arrived]))
+        rest_second = along_lines(jnp.concatenate([a[:, split:q_width] for a in arrived]))
+        kv_weights = [gathered(own_slices, q_width, [0]), gathered(rest_kv, 0, others)]
         q_weights = [
-            [gathered(own_slices, 0, [0]), gathered(rest_first, 0, others)],
-            [gathered(own_slices, split, [0])] + from_ring(rest_second, others),
+            [gathered(own_slices, 0, [0])] + from_lines(rest_first, others),
+            [gathered(own_slices, split, [0]), gathered(rest_second, 0, others)],
         ]
 
         both = ("ca", "tp")
@@ -299,11 +295,21 @@
         def swap(block):
             return lax.ppermute(block, both, [(i * 2 + c, i * 2 + 1 - c) for i in devices for c in range(2)])
 
-        own_half = lax.dynamic_slice_in_dim(tokens, core * half, half, 0)
-        near = cross(own_half, (1, 2))
-        other = cross(own_half, (2, 1))
-        far = cross(near, (2, 1))
-        for block, steps in ((near, (1, 2)), (other, (2, 1)), (far, (3, 3))):
+        begin = core * half
+
+        def share_tokens(tokens):
+            own_half = lax.dynamic_slice_in_dim(tokens, begin, half, 0)
+            near = cross(own_half, (1, 2))
+            other = cross(own_half, (2, 1))
+            far = cross(near, (2, 1))
+            return tuple((block, swap(block)) for block in (near, other, far))
+
+        def no_tokens(tokens):
+            return tuple((jnp.zeros((half, depth), tokens.dtype),) * 2 for _ in range(3))
+
+        known = sum(a[0, 0].astype(jnp.float32) for a in arrived)
+        blocks = lax.cond(known == known, share_tokens, no_tokens, tokens)
+        for (block, other_half), steps in zip(blocks, ((1, 2), (2, 1), (3, 3))):
 
             def here(s, steps=steps):
                 return (s[0] ^ jnp.where(s[2] == 0, steps[0], steps[1])) * row_count + s[2] * half
@@ -311,7 +317,7 @@
             def mate(s, steps=steps):
                 return (s[0] ^ jnp.where(s[2] == 0, steps[1], steps[0])) * row_count + (1 - s[2]) * half
 
-            token_parts += [(block, [here]), (swap(block), [mate])]
+            token_parts += [(block, [here]), (other_half, [mate])]
     else:
         split = q_width
         kv_weights = [gathered(own_slices, q_width, [0])]

time: 311 us -> 314 us (level)
  the two profiles are of different devices: /device:TPU:10 before, /device:TPU:16 now
where the time goes in v2:
time: 314 us; the launch traced here: 312 us
  waiting for transfers between devices  148 us (47%)
  Pallas kernels  88.6 us (28%)
  local copies, waits for them, and re-layouts  25.4 us (8%)
  starting transfers between devices  25.3 us (8%)
  between operations  15.6 us (5%)
  other arithmetic  8.83 us (3%)
    ppermute x3, waiting for transfers between devices, cross(): return lax.ppermute(block, both, pairs)  70.6 us
    ppermute x3, waiting for transfers between devices, directly(): return [block] + [lax.ppermute(block, 'ca', pairs) for pairs in shifts]  49.2 us
    pallas_call x8, Pallas kernels, attend(): pl.pallas_call(kernel, out_shape=jax.ShapeDtypeStruct((chunk_rows, width)...  47 us
    pallas_call x3, Pallas kernels, project(): pl.pallas_call(functools.partial(project_kernel, rope_heads, layout, base...  41.6 us
    ppermute x9, waiting for transfers between devices, to_partner(): return lax.ppermute(block, 'ca', [(i, i ^ step) for i in devices])  23.7 us
    ppermute x9, starting transfers between devices, to_partner(): return lax.ppermute(block, 'ca', [(i, i ^ step) for i in devices])  15.1 us
    unnamed x44, local copies, waits for them, and re-layouts  9.59 us
    gather x8, local copies, waits for them, and re-layouts, attend(): bounds = jnp.stack([places, starts[places], starts[places + TILE - 1]])  7.78 us
  transfers between devices with their start and end apart: 22, of which 10 were waited for; matrix products, arithmetic and copies ran while one was open for 7% of the time, Pallas kernels for 27%

profile of v2, /device:TPU:16, one launch (start us, length us, event | category | flops | bytes accessed | tf_op | source)
XLA Modules:
  0.0 311.8 jit_solution(18114414029708070617)
XLA Ops:
  8.9 2.5 collective-permute-start.8
  12.7 9.2 %collective-permute-done.8 = bf16[256,768]{1,0:T(8,128)(2,1)S(1)} collective-permute-done((bf16[256,768]{1,0:T(8,128)(2,1)S(1)}, bf16[256,768]{1,0:T(8,128)(2,1)S(1)}, u32[]{:S(2)}, u32[]{:S(2)}) %collective-permute-start.8) | collective-permute-done | bytes 393248 | tf_op jit(solution)/shard_map/ppermute | solution.py:236
  22.0 7.2 %collective-permute-done.7 = bf16[256,768]{1,0:T(8,128)(2,1)S(1)} collective-permute-done((bf16[256,768]{1,0:T(8,128)(2,1)S(1)}, bf16[256,768]{1,0:T(8,128)(2,1)S(1)}, u32[]{:S(2)}, u32[]{:S(2)}) %collective-permute-start.7) | collective-permute-done | bytes 393248 | tf_op jit(solution)/shard_map/ppermute | solution.py:236
  41.0 3.7 %fusion = (f32[2048,64]{1,0:T(8,128)S(1)}, f32[2048,64]{1,0:T(8,128)S(1)}, f32[2048,64]{1,0:T(8,128)S(1)}) fusion(f32[64]{0:T(128)S(1)} %multiply_power_fusion, f32[2048]{0:T(1024)S(1)} %get-tuple-element.49), kind=kLoop, calls=%fused_computation.20 | loop fusion | flops 262144 | bytes 1581312 | tf_op jit(solution)/shard_map/neg | solution.py:32
  44.7 1.6 pad_maximum_fusion
  50.5 81.0 %conditional.1 = (bf16[256,4096]{1,0:T(8,128)(2,1)}, bf16[256,4096]{1,0:T(8,128)(2,1)}, bf16[256,4096]{1,0:T(8,128)(2,1)}, bf16[256,4096]{1,0:T(8,128)(2,1)}, bf...) conditional(s32[]{:T(128)} %bitcast.9, () %tuple.13, (s32[]{:T(128)}, bf16[512,4096]{1,0:T(8,128)(2,1)}) %tuple.14), branch_computations={%region_2.3_spmd, %region_3.4_spmd} | conditional | flops 4 | bytes 54526288 | solution.py:311
  50.5 1.7 constant_dynamic-slice_fusion
  54.7 45.9 %collective-permute-done = bf16[256,4096]{1,0:T(8,128)(2,1)} collective-permute-done((bf16[256,4096]{1,0:T(8,128)(2,1)S(1)}, bf16[256,4096]{1,0:T(8,128)(2,1)}, u32[]{:S(2)}, u32[]{:S(2)}) %collective-permute-start) | collective-permute-done | bytes 2097184 | tf_op jit(solution)/shard_map/cond/branch_1_fun/ppermute | solution.py:293
  102.3 24.7 %collective-permute-done.4 = bf16[256,4096]{1,0:T(8,128)(2,1)} collective-permute-done((bf16[256,4096]{1,0:T(8,128)(2,1)}, bf16[256,4096]{1,0:T(8,128)(2,1)}, u32[]{:S(2)}, u32[]{:S(2)}) %collective-permute-start.4) | collective-permute-done | bytes 2097184 | tf_op jit(solution)/shard_map/cond/branch_1_fun/ppermute | solution.py:293
  127.0 4.5 %collective-permute-done.5 = bf16[256,4096]{1,0:T(8,128)(2,1)} collective-permute-done((bf16[256,4096]{1,0:T(8,128)(2,1)}, bf16[256,4096]{1,0:T(8,128)(2,1)}, u32[]{:S(2)}, u32[]{:S(2)}) %collective-permute-start.5) | collective-permute-done | bytes 2097184 | tf_op jit(solution)/shard_map/cond/branch_1_fun/ppermute | solution.py:296
  134.1 14.1 %shard_map.56.kv_ref = bf16[2048,256]{1,0:T(8,128)(2,1)S(1)} custom-call(s32[3]{0:T(128)S(1)} %pad_add_fusion.4.place, bf16[512,4096]{1,0:T(8,128)(2,1)} %refs_0_.5, bf16[256,4096]{1,0:T(8,128)(2,1)} %get-tuple-element.19.refs_1_, bf16[256,4096]{1,0:T(8,128)(2,1)} %get-tuple-element.20.refs_2_, bf16[256,4096]{1,0:T(8,128)(2,1)} %get-tuple-element.21.refs_3_, ...), custom_call_target="tpu_custom_call" | custom-call | flops 524288 | bytes 524288 | tf_op jit(solution)/shard_map/pallas_call | solution.py:93
  149.3 3.5 %collective-permute-start.12 = (bf16[1536,256]{1,0:T(8,128)(2,1)}, bf16[1536,256]{1,0:T(8,128)(2,1)S(1)}, u32[]{:S(2)}, u32[]{:S(2)}) collective-permute-start(bf16[1536,256]{1,0:T(8,128)(2,1)} %slice.77), channel_id=1, source_target_pairs={{0,8},{2,10},{4,12},{6,14},{8,16},{10,18},{12,20},{14,22},{16,24},... | collective-permute-start | bytes 2359304 | tf_op jit(solution)/shard_map/ppermute | solution.py:338
  153.7 1.6 collective-permute-start.9
  155.5 24.8 %collective-permute-done.10.refs_10_ = bf16[768,256]{1,0:T(8,128)(2,1)S(1)} collective-permute-done((bf16[768,256]{1,0:T(8,128)(2,1)S(1)}, bf16[768,256]{1,0:T(8,128)(2,1)S(1)}, u32[]{:S(2)}, u32[]{:S(2)}) %collective-permute-start.10) | collective-permute-done | bytes 393248 | tf_op jit(solution)/shard_map/ppermute | solution.py:245
  180.2 6.8 %collective-permute-done.11.refs_11_ = bf16[768,256]{1,0:T(8,128)(2,1)S(1)} collective-permute-done((bf16[768,256]{1,0:T(8,128)(2,1)S(1)}, bf16[768,256]{1,0:T(8,128)(2,1)S(1)}, u32[]{:S(2)}, u32[]{:S(2)}) %collective-permute-start.11) | collective-permute-done | bytes 393248 | tf_op jit(solution)/shard_map/ppermute | solution.py:245
  187.1 17.7 %collective-permute-done.9.refs_9_ = bf16[768,256]{1,0:T(8,128)(2,1)S(1)} collective-permute-done((bf16[768,256]{1,0:T(8,128)(2,1)S(1)}, bf16[768,256]{1,0:T(8,128)(2,1)S(1)}, u32[]{:S(2)}, u32[]{:S(2)}) %collective-permute-start.9) | collective-permute-done | bytes 393248 | tf_op jit(solution)/shard_map/ppermute | solution.py:245
  204.7 13.6 %shard_map.55.q_ref = bf16[2048,256]{1,0:T(8,128)(2,1)S(1)} custom-call(s32[3]{0:T(128)S(1)} %pad_add_fusion.4.place, bf16[512,4096]{1,0:T(8,128)(2,1)S(1)} %copy-done.10, bf16[256,4096]{1,0:T(8,128)(2,1)} %get-tuple-element.19.refs_1_, bf16[256,4096]{1,0:T(8,128)(2,1)} %get-tuple-element.20.refs_2_, bf16[256,4096]{1,0:T(8,128)(2,1)} %get-tuple-element.21.refs_3_, ...), custom_call_target="tpu_custom_call" | custom-call | flops 524288 | bytes 524288 | tf_op jit(solution)/shard_map/pallas_call | solution.py:93
  223.1 13.9 %shard_map.61.q_ref = bf16[2048,256]{1,0:T(8,128)(2,1)S(1)} custom-call(s32[3]{0:T(128)S(1)} %pad_add_fusion.4.place, bf16[512,4096]{1,0:T(8,128)(2,1)} %refs_0_.5, bf16[256,4096]{1,0:T(8,128)(2,1)} %get-tuple-element.19.refs_1_, bf16[256,4096]{1,0:T(8,128)(2,1)} %get-tuple-element.20.refs_2_, bf16[256,4096]{1,0:T(8,128)(2,1)} %get-tuple-element.21.refs_3_, ...), custom_call_target="tpu_custom_call" | custom-call | flops 524288 | bytes 524288 | tf_op jit(solution)/shard_map/pallas_call | solution.py:93
  237.0 4.2 %shard_map.64 = bf16[512,256]{1,0:T(8,128)(2,1)S(1)} custom-call(s32[3,2]{1,0:T(4,128)S(1)} %pad_add_fusion.2.bounds, bf16[2048,256]{1,0:T(8,128)(2,1)S(1)} %shard_map.61.q_ref, s32[2048,1]{1,0:T(8,128)S(1)} %copy.14.start_ref, bf16[1536,256]{1,0:T(8,128)(2,1)S(1)} %collective-permute-done.12.halo_ref, bf16[2048,256]{1,0:T(8,128)(2,1)S(1)} %shard_map.56.kv_ref), custom_call_target="tpu_custom_call" | custom-call | flops 536870912 | bytes 524288 | tf_op jit(solution)/shard_map/pallas_call | solution.py:184
  241.3 4.5 %collective-permute-start.18 = (bf16[512,256]{1,0:T(8,128)(2,1)S(1)}, bf16[512,256]{1,0:T(8,128)(2,1)S(1)}, u32[]{:S(2)}, u32[]{:S(2)}) collective-permute-start(bf16[512,256]{1,0:T(8,128)(2,1)S(1)} %shard_map.64), channel_id=1, source_target_pairs={{0,2},{2,0},{4,6},{6,4},{8,10},{10,8},{12,14},{14,12},{16,18},{18,... | collective-permute-start | bytes 786440 | tf_op jit(solution)/shard_map/ppermute | solution.py:236
  245.8 5.7 %shard_map.57 = bf16[512,256]{1,0:T(8,128)(2,1)S(1)} custom-call(s32[3,2]{1,0:T(4,128)S(1)} %get-tuple-element.51.bounds, bf16[2048,256]{1,0:T(8,128)(2,1)S(1)} %copy-done.1, s32[2048,1]{1,0:T(8,128)S(1)} %copy.14.start_ref, bf16[1536,256]{1,0:T(8,128)(2,1)S(1)} %collective-permute-done.12.halo_ref, bf16[2048,256]{1,0:T(8,128)(2,1)S(1)} %shard_map.56.kv_ref), custom_call_target="tpu_custom_call" | custom-call | flops 536870912 | bytes 524288 | tf_op jit(solution)/shard_map/pallas_call | solution.py:184
  251.5 1.7 collective-permute-start.13
  253.2 6.2 %shard_map.63 = bf16[512,256]{1,0:T(8,128)(2,1)S(1)} custom-call(s32[3,2]{1,0:T(4,128)S(1)} %get-tuple-element.52.bounds, bf16[2048,256]{1,0:T(8,128)(2,1)S(1)} %shard_map.61.q_ref, s32[2048,1]{1,0:T(8,128)S(1)} %copy.14.start_ref, bf16[1536,256]{1,0:T(8,128)(2,1)S(1)} %collective-permute-done.12.halo_ref, bf16[2048,256]{1,0:T(8,128)(2,1)S(1)} %shard_map.56.kv_ref), custom_call_target="tpu_custom_call" | custom-call | flops 536870912 | bytes 524288 | tf_op jit(solution)/shard_map/pallas_call | solution.py:184
  259.5 1.6 collective-permute-start.17
  261.1 4.0 %shard_map.59 = bf16[512,256]{1,0:T(8,128)(2,1)S(1)} custom-call(s32[3,2]{1,0:T(4,128)S(1)} %pad_add_fusion.2.bounds, bf16[2048,256]{1,0:T(8,128)(2,1)S(1)} %copy-done.1, s32[2048,1]{1,0:T(8,128)S(1)} %copy.14.start_ref, bf16[1536,256]{1,0:T(8,128)(2,1)S(1)} %collective-permute-done.12.halo_ref, bf16[2048,256]{1,0:T(8,128)(2,1)S(1)} %shard_map.56.kv_ref), custom_call_target="tpu_custom_call" | custom-call | flops 536870912 | bytes 524288 | tf_op jit(solution)/shard_map/pallas_call | solution.py:184
  265.1 1.6 collective-permute-start.15
  266.7 6.2 %shard_map.58 = bf16[512,256]{1,0:T(8,128)(2,1)S(1)} custom-call(s32[3,2]{1,0:T(4,128)S(1)} %get-tuple-element.52.bounds, bf16[2048,256]{1,0:T(8,128)(2,1)S(1)} %copy-done.1, s32[2048,1]{1,0:T(8,128)S(1)} %copy.14.start_ref, bf16[1536,256]{1,0:T(8,128)(2,1)S(1)} %collective-permute-done.12.halo_ref, bf16[2048,256]{1,0:T(8,128)(2,1)S(1)} %shard_map.56.kv_ref), custom_call_target="tpu_custom_call" | custom-call | flops 536870912 | bytes 524288 | tf_op jit(solution)/shard_map/pallas_call | solution.py:184
  272.9 2.0 collective-permute-start.14
  274.9 5.7 %shard_map.62 = bf16[512,256]{1,0:T(8,128)(2,1)S(1)} custom-call(s32[3,2]{1,0:T(4,128)S(1)} %get-tuple-element.51.bounds, bf16[2048,256]{1,0:T(8,128)(2,1)S(1)} %shard_map.61.q_ref, s32[2048,1]{1,0:T(8,128)S(1)} %copy.14.start_ref, bf16[1536,256]{1,0:T(8,128)(2,1)S(1)} %collective-permute-done.12.halo_ref, bf16[2048,256]{1,0:T(8,128)(2,1)S(1)} %shard_map.56.kv_ref), custom_call_target="tpu_custom_call" | custom-call | flops 536870912 | bytes 524288 | tf_op jit(solution)/shard_map/pallas_call | solution.py:184
  280.6 7.4 %shard_map.65 = bf16[512,256]{1,0:T(8,128)(2,1)S(1)} custom-call(s32[3,2]{1,0:T(4,128)S(1)} %pad_add_fusion.3.bounds, bf16[2048,256]{1,0:T(8,128)(2,1)S(1)} %shard_map.61.q_ref, s32[2048,1]{1,0:T(8,128)S(1)} %copy.14.start_ref, bf16[1536,256]{1,0:T(8,128)(2,1)S(1)} %collective-permute-done.12.halo_ref, bf16[2048,256]{1,0:T(8,128)(2,1)S(1)} %shard_map.56.kv_ref), custom_call_target="tpu_custom_call" | custom-call | flops 536870912 | bytes 524288 | tf_op jit(solution)/shard_map/pallas_call | solution.py:184
  288.1 7.4 %shard_map.60 = bf16[512,256]{1,0:T(8,128)(2,1)S(1)} custom-call(s32[3,2]{1,0:T(4,128)S(1)} %pad_add_fusion.3.bounds, bf16[2048,256]{1,0:T(8,128)(2,1)S(1)} %copy-done.1, s32[2048,1]{1,0:T(8,128)S(1)} %copy.14.start_ref, bf16[1536,256]{1,0:T(8,128)(2,1)S(1)} %collective-permute-done.12.halo_ref, bf16[2048,256]{1,0:T(8,128)(2,1)S(1)} %shard_map.56.kv_ref), custom_call_target="tpu_custom_call" | custom-call | flops 536870912 | bytes 524288 | tf_op jit(solution)/shard_map/pallas_call | solution.py:184
  296.0 7.1 %collective-permute-done.16 = bf16[512,256]{1,0:T(8,128)(2,1)S(1)} collective-permute-done((bf16[512,256]{1,0:T(8,128)(2,1)S(1)}, bf16[512,256]{1,0:T(8,128)(2,1)S(1)}, u32[]{:S(2)}, u32[]{:S(2)}) %collective-permute-start.16) | collective-permute-done | bytes 262176 | tf_op jit(solution)/shard_map/ppermute | solution.py:236
  (135 shorter events, 33.8 us)
Async XLA Ops:
  6.5 124.9 %all-gather.4.cloned.1.call-start = ((), (), s32[]{:S(2)}) async-start(), calls=%async_computation | async-start | bytes 1966080 | tf_op jit(solution)/shard_map/all_gather | solution.py:240
  8.8 122.6 %all-gather.6.cloned.1.call-start = ((), (), s32[]{:S(2)}) async-start(), calls=%async_computation.1 | async-start | bytes 1966080 | tf_op jit(solution)/shard_map/all_gather | solution.py:240
  8.9 13.0 %collective-permute-start.8 = (bf16[256,768]{1,0:T(8,128)(2,1)S(1)}, bf16[256,768]{1,0:T(8,128)(2,1)S(1)}, u32[]{:S(2)}, u32[]{:S(2)}) collective-permute-start(bf16[256,768]{1,0:T(8,128)(2,1)S(1)} %pad_maximum_fusion.4), channel_id=1, source_target_pairs={{0,6},{2,4},{4,2},{6,0},{8,14},{10,12},{12,10},{14,8},{16,22},{18,... | collective-permute-start | bytes 1179656 | tf_op jit(solution)/shard_map/ppermute | solution.py:236
  11.5 17.7 %collective-permute-start.7 = (bf16[256,768]{1,0:T(8,128)(2,1)S(1)}, bf16[256,768]{1,0:T(8,128)(2,1)S(1)}, u32[]{:S(2)}, u32[]{:S(2)}) collective-permute-start(bf16[256,768]{1,0:T(8,128)(2,1)S(1)} %pad_maximum_fusion.3), channel_id=1, source_target_pairs={{0,4},{2,6},{4,0},{6,2},{8,12},{10,14},{12,8},{14,10},{16,20},{18,... | collective-permute-start | bytes 1179656 | tf_op jit(solution)/shard_map/ppermute | solution.py:236
  12.1 18.9 %copy-start.21 = (s32[8]{0:T(128)S(1)}, s32[8]{0:T(128)}, u32[]{:S(2)}) copy-start(s32[8]{0:T(128)} %param.8) | copy-start | bytes 100
  12.1 17.2 %collective-permute-start.6 = (bf16[256,768]{1,0:T(8,128)(2,1)S(1)}, bf16[256,768]{1,0:T(8,128)(2,1)S(1)}, u32[]{:S(2)}, u32[]{:S(2)}) collective-permute-start(bf16[256,768]{1,0:T(8,128)(2,1)S(1)} %pad_maximum_fusion.2), channel_id=1, source_target_pairs={{0,2},{2,0},{4,6},{6,4},{8,10},{10,8},{12,14},{14,12},{16,18},{18,... | collective-permute-start | bytes 1179656 | tf_op jit(solution)/shard_map/ppermute | solution.py:236
  30.9 188.4 %all-gather.8.cloned.1.call-start = ((), (), s32[]{:S(2)}) async-start(), calls=%async_computation.2 | async-start | bytes 1966080 | tf_op jit(solution)/shard_map/all_gather | solution.py:240
  46.3 85.2 %copy-start.2 = (f32[2048,128]{1,0:T(8,128)}, f32[2048,128]{1,0:T(8,128)S(1)}, u32[]{:S(2)}) copy-start(f32[2048,128]{1,0:T(8,128)S(1)} %get-tuple-element.61.refs_12_.refs_9_) | copy-start | bytes 3145732
  52.3 48.3 %collective-permute-start = (bf16[256,4096]{1,0:T(8,128)(2,1)S(1)}, bf16[256,4096]{1,0:T(8,128)(2,1)}, u32[]{:S(2)}, u32[]{:S(2)}) collective-permute-start(bf16[256,4096]{1,0:T(8,128)(2,1)S(1)} %constant_dynamic-slice_fusion), channel_id=1, source_target_pairs={{0,2},{1,5},{2,0},{3,7},{4,6},{5,1},{6,4},{7,3},{8,10},{9,13},{10,... | collective-permute-start | bytes 6291464 | tf_op jit(solution)/shard_map/cond/branch_1_fun/ppermute | solution.py:293
  53.8 48.0 %collective-permute-start.2 = (bf16[256,4096]{1,0:T(8,128)(2,1)S(1)}, bf16[256,4096]{1,0:T(8,128)(2,1)}, u32[]{:S(2)}, u32[]{:S(2)}) collective-permute-start(bf16[256,4096]{1,0:T(8,128)(2,1)S(1)} %constant_dynamic-slice_fusion), channel_id=1, source_target_pairs={{0,4},{1,3},{2,6},{3,1},{4,0},{5,7},{6,2},{7,5},{8,12},{9,11},{10,... | collective-permute-start | bytes 6291464 | tf_op jit(solution)/shard_map/cond/branch_1_fun/ppermute | solution.py:293
  100.6 26.4 %collective-permute-start.4 = (bf16[256,4096]{1,0:T(8,128)(2,1)}, bf16[256,4096]{1,0:T(8,128)(2,1)}, u32[]{:S(2)}, u32[]{:S(2)}) collective-permute-start(bf16[256,4096]{1,0:T(8,128)(2,1)} %collective-permute-done), channel_id=1, source_target_pairs={{0,4},{1,3},{2,6},{3,1},{4,0},{5,7},{6,2},{7,5},{8,12},{9,11},{10,... | collective-permute-start | bytes 6291464 | tf_op jit(solution)/shard_map/cond/branch_1_fun/ppermute | solution.py:293
  101.8 25.2 %collective-permute-start.1 = (bf16[256,4096]{1,0:T(8,128)(2,1)}, bf16[256,4096]{1,0:T(8,128)(2,1)}, u32[]{:S(2)}, u32[]{:S(2)}) collective-permute-start(bf16[256,4096]{1,0:T(8,128)(2,1)} %collective-permute-done), channel_id=1, source_target_pairs={{0,1},{1,0},{2,3},{3,2},{4,5},{5,4},{6,7},{7,6},{8,9},{9,8},{10,11... | collective-permute-start | bytes 6291464 | tf_op jit(solution)/shard_map/cond/branch_1_fun/ppermute | solution.py:296
  101.8 25.2 %collective-permute-start.3 = (bf16[256,4096]{1,0:T(8,128)(2,1)}, bf16[256,4096]{1,0:T(8,128)(2,1)}, u32[]{:S(2)}, u32[]{:S(2)}) collective-permute-start(bf16[256,4096]{1,0:T(8,128)(2,1)} %collective-permute-done.2), channel_id=1, source_target_pairs={{0,1},{1,0},{2,3},{3,2},{4,5},{5,4},{6,7},{7,6},{8,9},{9,8},{10,11... | collective-permute-start | bytes 6291464 | tf_op jit(solution)/shard_map/cond/branch_1_fun/ppermute | solution.py:296
  127.0 4.5 %collective-permute-start.5 = (bf16[256,4096]{1,0:T(8,128)(2,1)}, bf16[256,4096]{1,0:T(8,128)(2,1)}, u32[]{:S(2)}, u32[]{:S(2)}) collective-permute-start(bf16[256,4096]{1,0:T(8,128)(2,1)} %collective-permute-done.4), channel_id=1, source_target_pairs={{0,1},{1,0},{2,3},{3,2},{4,5},{5,4},{6,7},{7,6},{8,9},{9,8},{10,11... | collective-permute-start | bytes 6291464 | tf_op jit(solution)/shard_map/cond/branch_1_fun/ppermute | solution.py:296
  134.1 70.6 %copy-start.10 = (bf16[512,4096]{1,0:T(8,128)(2,1)S(1)}, bf16[512,4096]{1,0:T(8,128)(2,1)}, u32[]{:S(2)}) copy-start(bf16[512,4096]{1,0:T(8,128)(2,1)} %refs_0_.5) | copy-start | bytes 12582916
  148.3 7.1 %copy-start.16 = (s32[2]{0:T(128)S(1)}, s32[2]{0:T(128)}, u32[]{:S(2)}) copy-start(s32[2]{0:T(128)} %gather_fusion.6) | copy-start | bytes 28
  148.3 7.1 %copy-start.18 = (s32[2]{0:T(128)S(1)}, s32[2]{0:T(128)}, u32[]{:S(2)}) copy-start(s32[2]{0:T(128)} %gather_fusion.4) | copy-start | bytes 28
  148.3 7.1 %copy-start.19 = (s32[2]{0:T(128)S(1)}, s32[2]{0:T(128)}, u32[]{:S(2)}) copy-start(s32[2]{0:T(128)} %gather_fusion.5) | copy-start | bytes 28
  148.3 7.1 %copy-start.15 = (s32[2]{0:T(128)S(1)}, s32[2]{0:T(128)}, u32[]{:S(2)}) copy-start(s32[2]{0:T(128)} %gather_fusion.1) | copy-start | bytes 28
  148.3 56.4 %copy-start.3 = (f32[2048,128]{1,0:T(8,128)S(1)}, f32[2048,128]{1,0:T(8,128)}, u32[]{:S(2)}) copy-start(f32[2048,128]{1,0:T(8,128)} %copy-done.2) | copy-start | bytes 3145732
  148.3 56.4 %copy-start.6 = (f32[2048,128]{1,0:T(8,128)S(1)}, f32[2048,128]{1,0:T(8,128)}, u32[]{:S(2)}) copy-start(f32[2048,128]{1,0:T(8,128)} %get-tuple-element.62.refs_13_.refs_10_) | copy-start | bytes 3145732
  149.3 87.7 %collective-permute-start.12 = (bf16[1536,256]{1,0:T(8,128)(2,1)}, bf16[1536,256]{1,0:T(8,128)(2,1)S(1)}, u32[]{:S(2)}, u32[]{:S(2)}) collective-permute-start(bf16[1536,256]{1,0:T(8,128)(2,1)} %slice.77), channel_id=1, source_target_pairs={{0,8},{2,10},{4,12},{6,14},{8,16},{10,18},{12,20},{14,22},{16,24},... | collective-permute-start | bytes 2359304 | tf_op jit(solution)/shard_map/ppermute | solution.py:338
  152.8 27.4 %collective-permute-start.10 = (bf16[768,256]{1,0:T(8,128)(2,1)S(1)}, bf16[768,256]{1,0:T(8,128)(2,1)S(1)}, u32[]{:S(2)}, u32[]{:S(2)}) collective-permute-start(bf16[768,256]{1,0:T(8,128)(2,1)S(1)} %pad_maximum_fusion.6.refs_8_), channel_id=1, source_target_pairs={{0,16},{2,18},{4,20},{6,22},{8,24},{10,26},{12,28},{14,30},{16,0},... | collective-permute-start | bytes 1179656 | tf_op jit(solution)/shard_map/ppermute | solution.py:245
  153.3 33.7 %collective-permute-start.11 = (bf16[768,256]{1,0:T(8,128)(2,1)S(1)}, bf16[768,256]{1,0:T(8,128)(2,1)S(1)}, u32[]{:S(2)}, u32[]{:S(2)}) collective-permute-start(bf16[768,256]{1,0:T(8,128)(2,1)S(1)} %pad_maximum_fusion.6.refs_8_), channel_id=1, source_target_pairs={{0,24},{2,26},{4,28},{6,30},{8,0},{10,2},{12,4},{14,6},{16,8},{18,... | collective-permute-start | bytes 1179656 | tf_op jit(solution)/shard_map/ppermute | solution.py:245
  153.7 51.0 %collective-permute-start.9 = (bf16[768,256]{1,0:T(8,128)(2,1)S(1)}, bf16[768,256]{1,0:T(8,128)(2,1)S(1)}, u32[]{:S(2)}, u32[]{:S(2)}) collective-permute-start(bf16[768,256]{1,0:T(8,128)(2,1)S(1)} %pad_maximum_fusion.6.refs_8_), channel_id=1, source_target_pairs={{0,8},{2,10},{4,12},{6,14},{8,16},{10,18},{12,20},{14,22},{16,24},... | collective-permute-start | bytes 1179656 | tf_op jit(solution)/shard_map/ppermute | solution.py:245
  237.0 8.8 %copy-start.1 = (bf16[2048,256]{1,0:T(8,128)(2,1)S(1)}, bf16[2048,256]{1,0:T(8,128)(2,1)}, u32[]{:S(2)}) copy-start(bf16[2048,256]{1,0:T(8,128)(2,1)} %copy-done) | copy-start | bytes 3145732
  241.3 61.9 %collective-permute-start.18 = (bf16[512,256]{1,0:T(8,128)(2,1)S(1)}, bf16[512,256]{1,0:T(8,128)(2,1)S(1)}, u32[]{:S(2)}, u32[]{:S(2)}) collective-permute-start(bf16[512,256]{1,0:T(8,128)(2,1)S(1)} %shard_map.64), channel_id=1, source_target_pairs={{0,2},{2,0},{4,6},{6,4},{8,10},{10,8},{12,14},{14,12},{16,18},{18,... | collective-permute-start | bytes 786440 | tf_op jit(solution)/shard_map/ppermute | solution.py:236
  251.5 43.9 %collective-permute-start.13 = (bf16[512,256]{1,0:T(8,128)(2,1)S(1)}, bf16[512,256]{1,0:T(8,128)(2,1)S(1)}, u32[]{:S(2)}, u32[]{:S(2)}) collective-permute-start(bf16[512,256]{1,0:T(8,128)(2,1)S(1)} %shard_map.57), channel_id=1, source_target_pairs={{0,6},{2,4},{4,2},{6,0},{8,14},{10,12},{12,10},{14,8},{16,22},{18,... | collective-permute-start | bytes 786440 | tf_op jit(solution)/shard_map/ppermute | solution.py:236
  259.5 43.7 %collective-permute-start.17 = (bf16[512,256]{1,0:T(8,128)(2,1)S(1)}, bf16[512,256]{1,0:T(8,128)(2,1)S(1)}, u32[]{:S(2)}, u32[]{:S(2)}) collective-permute-start(bf16[512,256]{1,0:T(8,128)(2,1)S(1)} %shard_map.63), channel_id=1, source_target_pairs={{0,4},{2,6},{4,0},{6,2},{8,12},{10,14},{12,8},{14,10},{16,20},{18,... | collective-permute-start | bytes 786440 | tf_op jit(solution)/shard_map/ppermute | solution.py:236
  265.1 30.8 %collective-permute-start.15 = (bf16[512,256]{1,0:T(8,128)(2,1)S(1)}, bf16[512,256]{1,0:T(8,128)(2,1)S(1)}, u32[]{:S(2)}, u32[]{:S(2)}) collective-permute-start(bf16[512,256]{1,0:T(8,128)(2,1)S(1)} %shard_map.59), channel_id=1, source_target_pairs={{0,2},{2,0},{4,6},{6,4},{8,10},{10,8},{12,14},{14,12},{16,18},{18,... | collective-permute-start | bytes 786440 | tf_op jit(solution)/shard_map/ppermute | solution.py:236
  272.9 23.0 %collective-permute-start.14 = (bf16[512,256]{1,0:T(8,128)(2,1)S(1)}, bf16[512,256]{1,0:T(8,128)(2,1)S(1)}, u32[]{:S(2)}, u32[]{:S(2)}) collective-permute-start(bf16[512,256]{1,0:T(8,128)(2,1)S(1)} %shard_map.58), channel_id=1, source_target_pairs={{0,4},{2,6},{4,0},{6,2},{8,12},{10,14},{12,8},{14,10},{16,20},{18,... | collective-permute-start | bytes 786440 | tf_op jit(solution)/shard_map/ppermute | solution.py:236
  295.5 7.6 %collective-permute-start.16 = (bf16[512,256]{1,0:T(8,128)(2,1)S(1)}, bf16[512,256]{1,0:T(8,128)(2,1)S(1)}, u32[]{:S(2)}, u32[]{:S(2)}) collective-permute-start(bf16[512,256]{1,0:T(8,128)(2,1)S(1)} %shard_map.62), channel_id=1, source_target_pairs={{0,6},{2,4},{4,2},{6,0},{8,14},{10,12},{12,10},{14,8},{16,22},{18,... | collective-permute-start | bytes 786440 | tf_op jit(solution)/shard_map/ppermute | solution.py:236
  (12 other events, 26.5 us)
Sparse Core Ops, SparseCore 0:
  9.0 37.0 all-gather.3
  47.6 35.9 all-gather.5
  85.2 35.9 all-gather.7
